TPU v7x, 512 devices: a whole 4x4x16 slice. The times are simulated.
512 devices in a mesh: dp: 32 (over z, core), seq: 16 (over x, y).
Axes of the slice: x: 4, y: 4, z: 16, core: 2. Of those that a mesh axis runs over, the one named last changes fastest.
Arguments:
- queries: bfloat16 [1024, 64, 1024], P('seq', 'dp'), may hold values from -8 to 8
- key_rows: bfloat16 [1024, 64, 1024], P('seq', 'dp'), may hold values from -8 to 8
- value_rows: bfloat16 [1024, 64, 1024], P('seq', 'dp'), may hold values from -6 to 6
- cotangent: bfloat16 [1024, 64, 1024], P('seq', 'dp'), may hold values from -6 to 6
- out_weight: bfloat16 [1024, 1024], P('seq'), may hold values from -0.1875 to 0.1875
- node_counts: int32 [64], P('dp'), may hold values from 256 to 1024, as said below
- edge_bits: int32 [64, 8, 1], P('dp'), may hold values from 0 to 255, as said below
Outputs:
- layer_out: bfloat16 [1024, 64, 1024], P('seq', 'dp')
- query_grad: bfloat16 [1024, 64, 1024], P('seq', 'dp')
- key_grad: bfloat16 [1024, 64, 1024], P('seq', 'dp')
- value_grad: bfloat16 [1024, 64, 1024], P('seq', 'dp')
- weight_grad: float32 [1024, 1024], P('seq')
Inputs may be any that keep to these rules, and one draw needn't show every extreme that they name: `node_counts`: every count is at least 256; some graph has exactly 1024. `edge_bits`: bits for blocks at or past 8 are 0; every query block sees its own key block and key block 0; in some graph the last query block sees every key block.
All inputs are finite; a program needn't handle non-finite values.
Results may differ from a plain program's by a relative error of at most 0.012.
The roundings to bfloat16 on the way count: a program that leaves them out, or rounds other values in their place, can miss the bound.
Values may be sent and summed in bfloat16 or wider, within the bound.
A program may use at most 64 MiB of HBM per device.

v0:
```python
import math

import jax
import jax.numpy as jnp
from jax import lax
from jax.sharding import PartitionSpec as P

HEAD_DIM = 128
BLOCK = 128
WORD_BITS = 16


def permitted(row_words, col_pos, amount):
    col_block = col_pos // BLOCK
    chosen = jnp.zeros((row_words.shape[0], col_pos.shape[0]), jnp.int32)
    chosen = jnp.where((col_block // WORD_BITS == 0)[None, :], row_words, chosen)
    flag_bits = jnp.right_shift(chosen, (col_block % WORD_BITS)[None, :]) & 1
    return (flag_bits == 1) & (col_pos < amount)[None, :]


def probabilities(query_part, key_all, row_words, amount, score_scale):
    col_pos = jnp.arange(key_all.shape[0], dtype=jnp.int32)
    scores = (
        lax.dot_general(
            query_part, key_all, (((1,), (1,)), ((), ())), preferred_element_type=jnp.float32
        )
        * score_scale
    )
    scores = jnp.where(permitted(row_words, col_pos, amount), scores, -jnp.inf)
    row_top = jnp.max(scores, axis=1, keepdims=True)
    weights = jnp.exp(scores - row_top)
    return weights / jnp.sum(weights, axis=1, keepdims=True)


def forward_rows(query_part, row_start, key_all, value_all, row_words, amount, score_scale):
    probability = probabilities(query_part, key_all, row_words, amount, score_scale)
    row_pos = row_start + jnp.arange(query_part.shape[0], dtype=jnp.int32)
    mixed = jnp.dot(probability.astype(jnp.bfloat16), value_all, preferred_element_type=jnp.float32)
    return jnp.where((row_pos < amount)[:, None], mixed, 0.0).astype(jnp.bfloat16)


def backward_rows(
    query_part, att_part, grad_part, key_all, value_all, row_words, amount, score_scale
):
    probability = probabilities(query_part, key_all, row_words, amount, score_scale)
    value_share = lax.dot_general(
        probability.astype(jnp.bfloat16),
        grad_part,
        (((0,), (0,)), ((), ())),
        preferred_element_type=jnp.float32,
    )
    prob_grad = lax.dot_general(
        grad_part, value_all, (((1,), (1,)), ((), ())), preferred_element_type=jnp.float32
    )
    centre = jnp.sum(
        grad_part.astype(jnp.float32) * att_part.astype(jnp.float32), axis=1, keepdims=True
    )
    score_grad = (probability * (prob_grad - centre) * score_scale).astype(jnp.bfloat16)
    query_share = jnp.dot(score_grad, key_all, preferred_element_type=jnp.float32)
    key_share = lax.dot_general(
        score_grad, query_part, (((0,), (0,)), ((), ())), preferred_element_type=jnp.float32
    )
    return (query_share, key_share, value_share)


def on_device(queries, key_rows, value_rows, cotangent, out_weight, node_counts, edge_bits):
    node_rows, graphs_here, feature_width = queries.shape
    head_size = HEAD_DIM
    head_count = feature_width // head_size
    seq_count = lax.axis_size("seq")
    data_count = lax.axis_size("dp")
    item_count = graphs_here * head_count
    item_share = item_count // seq_count
    node_total = node_rows * seq_count
    block_rows = min(512, node_total)
    block_total = node_total // block_rows
    score_scale = 1.0 / math.sqrt(head_size)
    first_item = lax.axis_index("seq") * item_share
    item_counts = lax.dynamic_slice_in_dim(
        jnp.repeat(node_counts, head_count), first_item, item_share
    )
    item_bits = lax.dynamic_slice_in_dim(
        jnp.repeat(edge_bits, head_count, axis=0), first_item, item_share, 0
    )

    def split_heads(values_in):
        return values_in.reshape(node_rows, item_count, head_size)

    def leading(values_in):
        return jnp.transpose(values_in, (1, 0, 2))

    query_heads, key_heads, value_heads = (
        lax.all_to_all(split_heads(queries), "seq", split_axis=1, concat_axis=0, tiled=True),
        lax.all_to_all(split_heads(key_rows), "seq", split_axis=1, concat_axis=0, tiled=True),
        lax.all_to_all(split_heads(value_rows), "seq", split_axis=1, concat_axis=0, tiled=True),
    )
    query_items = leading(query_heads)
    key_items = leading(key_heads)
    value_items = leading(value_heads)

    def forward_item(operands):
        query_all, key_all, value_all, amount, block_bits = operands
        row_words = jnp.repeat(block_bits, BLOCK, axis=0)

        def forward_one_block(block_index):
            row_start = block_index * block_rows
            query_part = lax.dynamic_slice_in_dim(query_all, row_start, block_rows)
            word_part = lax.dynamic_slice_in_dim(row_words, row_start, block_rows)
            return forward_rows(
                query_part, row_start, key_all, value_all, word_part, amount, score_scale
            )

        return lax.map(forward_one_block, jnp.arange(block_total, dtype=jnp.int32)).reshape(
            node_total, head_size
        )

    attended_items = lax.map(
        forward_item, (query_items, key_items, value_items, item_counts, item_bits)
    )
    attended_nodes = lax.all_to_all(
        leading(attended_items), "seq", split_axis=0, concat_axis=1, tiled=True
    )
    attended = attended_nodes.reshape(node_rows * graphs_here, feature_width)
    flat_cot = cotangent.reshape(node_rows * graphs_here, feature_width)
    row_pos = lax.axis_index("seq") * node_rows + jnp.arange(node_rows, dtype=jnp.int32)
    valid_rows = (row_pos[:, None] < node_counts[None, :]).reshape(-1, 1)
    full_weight = lax.all_gather(out_weight, "seq", axis=0, tiled=True)
    out_sum = jnp.dot(attended, full_weight, preferred_element_type=jnp.float32)
    back_sum = lax.dot_general(
        flat_cot, full_weight, (((1,), (1,)), ((), ())), preferred_element_type=jnp.float32
    )
    layer_out = out_sum.astype(jnp.bfloat16).reshape(node_rows, graphs_here, feature_width)
    att_grad = jnp.where(valid_rows, back_sum, 0.0).astype(jnp.bfloat16)
    grad_heads = lax.all_to_all(
        att_grad.reshape(node_rows, item_count, head_size),
        "seq",
        split_axis=1,
        concat_axis=0,
        tiled=True,
    )

    def backward_item(operands):
        query_all, key_all, value_all, att_all, grad_all, amount, block_bits = operands
        row_words = jnp.repeat(block_bits, BLOCK, axis=0)

        def backward_one_block(carried, block_index):
            key_sum, value_sum = carried
            row_start = block_index * block_rows

            def rows_of(values_in):
                return lax.dynamic_slice_in_dim(values_in, row_start, block_rows)

            query_share, key_share, value_share = backward_rows(
                rows_of(query_all),
                rows_of(att_all),
                rows_of(grad_all),
                key_all,
                value_all,
                rows_of(row_words),
                amount,
                score_scale,
            )
            return (
                (key_sum + key_share, value_sum + value_share),
                query_share.astype(jnp.bfloat16),
            )

        zeros_init = jnp.zeros((node_total, head_size), jnp.float32)
        (key_sum, value_sum), query_blocks = lax.scan(
            backward_one_block, (zeros_init, zeros_init), jnp.arange(block_total, dtype=jnp.int32)
        )
        return (
            query_blocks.reshape(node_total, head_size),
            key_sum.astype(jnp.bfloat16),
            value_sum.astype(jnp.bfloat16),
        )

    query_grad, key_grad, value_grad = lax.map(
        backward_item,
        (
            query_items,
            key_items,
            value_items,
            attended_items,
            leading(grad_heads),
            item_counts,
            item_bits,
        ),
    )
    back_query, back_key, back_value = (
        lax.all_to_all(leading(query_grad), "seq", split_axis=0, concat_axis=1, tiled=True),
        lax.all_to_all(leading(key_grad), "seq", split_axis=0, concat_axis=1, tiled=True),
        lax.all_to_all(leading(value_grad), "seq", split_axis=0, concat_axis=1, tiled=True),
    )

    def to_nodes(values_in):
        return values_in.reshape(node_rows, graphs_here, feature_width)

    grad_scale = 1.0 / math.sqrt(data_count * graphs_here * node_total)
    partial_grad = lax.psum_scatter(
        lax.dot_general(
            attended, flat_cot, (((0,), (0,)), ((), ())), preferred_element_type=jnp.float32
        )
        * grad_scale,
        "seq",
        scatter_dimension=0,
        tiled=True,
    )
    weight_grad = lax.psum(partial_grad, "dp")
    return (layer_out, to_nodes(back_query), to_nodes(back_key), to_nodes(back_value), weight_grad)


def solution(mesh):
    in_specs = (
        P("seq", "dp", None),
        P("seq", "dp", None),
        P("seq", "dp", None),
        P("seq", "dp", None),
        P("seq", None),
        P("dp"),
        P("dp", None, None),
    )
    out_specs = (
        P("seq", "dp", None),
        P("seq", "dp", None),
        P("seq", "dp", None),
        P("seq", "dp", None),
        P("seq", None),
    )
    return jax.shard_map(
        on_device, mesh=mesh, in_specs=in_specs, out_specs=out_specs, check_vma=False
    )
```

profile of v0, /device:TPU:1, one launch (start us, length us, event | category | flops | bytes accessed | tf_op | source)
XLA Modules:
  0.0 401.7 jit_solution(4827935351455443793)
XLA Ops:
  7.2 1.2 reshape.198
  8.4 0.8 copy.56
  9.1 7.6 %all-to-all-start = ((bf16[64,16,128]{2,0,1:T(8,128)(2,1)}), bf16[64,16,128]{2,0,1:T(8,128)(2,1)S(1)}, u32[]{:S(2)}, u32[]{:S(2)}) async-start(bf16[64,16,128]{2,0,1:T(8,128)(2,1)} %copy.56), calls=%async_computation | async-start | bytes 524288 | tf_op jit(solution)/shard_map/all_to_all | solution.py:93
  17.5 1.1 reshape.199
  18.6 0.8 copy.57
  19.4 4.8 %all-to-all-done = bf16[64,16,128]{2,0,1:T(8,128)(2,1)S(1)} async-done(((bf16[64,16,128]{2,0,1:T(8,128)(2,1)}), bf16[64,16,128]{2,0,1:T(8,128)(2,1)S(1)}, u32[]{:S(2)}, u32[]{:S(2)}) %all-to-all-start) | async-done | bytes 262176 | tf_op jit(solution)/shard_map/all_to_all | solution.py:93
  24.1 3.6 all-to-all-start.1
  27.9 0.8 copy.58
  28.7 6.4 %all-to-all-done.1 = bf16[64,16,128]{2,0,1:T(8,128)(2,1)S(1)} async-done(((bf16[64,16,128]{2,0,1:T(8,128)(2,1)}), bf16[64,16,128]{2,0,1:T(8,128)(2,1)S(1)}, u32[]{:S(2)}, u32[]{:S(2)}) %all-to-all-start.1) | async-done | bytes 262176 | tf_op jit(solution)/shard_map/all_to_all | solution.py:94
  35.1 3.5 all-to-all-start.2
  39.8 6.1 %all-to-all-done.2 = bf16[64,16,128]{2,0,1:T(8,128)(2,1)S(1)} async-done(((bf16[64,16,128]{2,0,1:T(8,128)(2,1)}), bf16[64,16,128]{2,0,1:T(8,128)(2,1)S(1)}, u32[]{:S(2)}, u32[]{:S(2)}) %all-to-all-start.2) | async-done | bytes 262176 | tf_op jit(solution)/shard_map/all_to_all | solution.py:95
  46.0 9.3 %while.49 = (s32[]{:T(128)}, bf16[2,512,128]{2,1,0:T(8,128)(2,1)S(1)}, s32[2]{0:T(128)S(1)}, s32[]{:T(128)}, s32[1024,1]{0,1:T(1,128)S(1)}, /*index=5*/bf16[1024...) while((s32[]{:T(128)}, ...), condition=%wide.region_3.4_spmd, body=%wide.region_0.3_spmd.sunk | while | flops 275427328 | bytes 7107791 | solution.py:113
  48.6 0.9 fusion.78
  53.3 0.9 fusion.78
  55.8 0.8 reduce.2
  56.6 0.8 reshape.209
  57.4 3.5 all-to-all-start.3
  61.1 7.1 %all-to-all-done.3 = bf16[16,2,4096]{2,1,0:T(2,128)(2,1)S(1)} async-done(((bf16[16,2,4096]{2,1,0:T(2,128)(2,1)}), bf16[16,2,4096]{2,1,0:T(2,128)(2,1)S(1)}, u32[]{:S(2)}, u32[]{:S(2)}) %all-to-all-start.3) | async-done | bytes 262176 | tf_op jit(solution)/shard_map/all_to_all | solution.py:120
  68.9 2.7 convolution_multiply_fusion
  71.8 13.2 %all-gather.2.cloned.1.call-done = bf16[1024,1024]{1,0:T(8,128)(2,1)} async-done(((bf16[64,1024]{1,0:T(8,128)(2,1)}), bf16[1024,1024]{1,0:T(8,128)(2,1)}) %all-gather.2.cloned.1.call-update) | async-done | bytes 2097168 | tf_op jit(solution)/shard_map/all_gather | solution.py:127
  85.0 2.4 fusion.40
  87.5 0.8 copy.61
  88.3 4.7 %all-to-all-start.4 = ((bf16[64,16,128]{2,0,1:T(8,128)(2,1)}), bf16[64,16,128]{2,0,1:T(8,128)(2,1)S(1)}, u32[]{:S(2)}, u32[]{:S(2)}) async-start(bf16[64,16,128]{2,0,1:T(8,128)(2,1)} %copy.61), calls=%async_computation.4 | async-start | bytes 524288 | tf_op jit(solution)/shard_map/all_to_all | solution.py:134
  93.0 7.3 %all-to-all-done.4 = bf16[64,16,128]{2,0,1:T(8,128)(2,1)S(1)} async-done(((bf16[64,16,128]{2,0,1:T(8,128)(2,1)}), bf16[64,16,128]{2,0,1:T(8,128)(2,1)S(1)}, u32[]{:S(2)}, u32[]{:S(2)}) %all-to-all-start.4) | async-done | bytes 262176 | tf_op jit(solution)/shard_map/all_to_all | solution.py:134
  100.3 12.5 %while.50 = (s32[]{:T(128)}, f32[1024,128]{1,0:T(8,128)S(1)}, f32[1024,128]{1,0:T(8,128)S(1)}, bf16[2,512,128]{2,1,0:T(8,128)(2,1)S(1)}, s32[2]{0:T(128)S(1)}, /...) while((s32[]{:T(128)}, f32[1024,128]{1,0:T(8,128)S(1)}, ...), condition=%wide.region_8.9_spmd.clone, body=%wide.region_4.8_spmd.clone.sunk | while | flops 681945600 | bytes 15372546 | solution.py:169
  102.4 0.9 fusion.91
  103.9 0.9 convolution_add_fusion.5
  108.7 0.9 fusion.91
  110.1 0.9 convolution_add_fusion.5
  111.0 0.7 multiply_convert_fusion.2
  112.9 0.8 reduce.3
  113.7 0.8 reshape.211
  114.5 3.7 all-to-all-start.5
  118.2 1.0 reduce.4
  119.2 0.8 reshape.213
  120.0 6.6 %all-to-all-done.5 = bf16[16,2,4096]{2,1,0:T(2,128)(2,1)S(1)} async-done(((bf16[16,2,4096]{2,1,0:T(2,128)(2,1)}), bf16[16,2,4096]{2,1,0:T(2,128)(2,1)S(1)}, u32[]{:S(2)}, u32[]{:S(2)}) %all-to-all-start.5) | async-done | bytes 262176 | tf_op jit(solution)/shard_map/all_to_all | solution.py:191
  126.5 3.5 all-to-all-start.6
  130.2 0.8 reduce.5
  131.0 0.8 reshape.215
  131.7 52.0 %reduce-scatter.2.cloned.1.call-done = f32[64,1024]{1,0:T(8,128)} async-done(((f32[1024,1024]{1,0:T(8,128)}), f32[64,1024]{1,0:T(8,128)}) %reduce-scatter.2.cloned.1.call-update) | async-done | bytes 262160 | tf_op jit(solution)/shard_map/reduce_scatter | solution.py:200
  183.7 4.7 %all-to-all-start.7 = ((bf16[16,2,4096]{2,1,0:T(2,128)(2,1)}), bf16[16,2,4096]{2,1,0:T(2,128)(2,1)S(1)}, u32[]{:S(2)}, u32[]{:S(2)}) async-start(bf16[16,2,4096]{2,1,0:T(2,128)(2,1)} %reshape.215), calls=%async_computation.7 | async-start | bytes 524288 | tf_op jit(solution)/shard_map/all_to_all | solution.py:193
  188.9 0.8 reshape.202
  190.2 0.8 reshape.205
  191.5 0.8 reshape.206
  192.3 3.6 all-to-all-done.7
  196.4 0.8 reshape.207
  197.2 196.3 %all-reduce.2.cloned.1.call-done = f32[64,1024]{1,0:T(8,128)} async-done(((f32[64,1024]{1,0:T(8,128)}), f32[64,1024]{1,0:T(8,128)}) %all-reduce.2.cloned.1.call-update) | async-done | bytes 262160 | tf_op jit(solution)/shard_map/psum | solution.py:209
  393.5 1.7 copy.97
  (84 shorter events, 18.7 us)
Async XLA Ops:
  7.2 20.6 %copy-start.1 = (bf16[64,2,1024]{2,1,0:T(2,128)(2,1)S(1)}, bf16[64,2,1024]{2,1,0:T(2,128)(2,1)}, u32[]{:S(2)}) copy-start(bf16[64,2,1024]{2,1,0:T(2,128)(2,1)} %param.13) | copy-start | bytes 786436
  8.3 30.3 %copy-start.4 = (s32[2]{0:T(128)S(1)}, s32[2]{0:T(128)}, u32[]{:S(2)}) copy-start(s32[2]{0:T(128)} %param.16) | copy-start | bytes 28
  8.4 30.4 %copy-start.3 = (s32[2,8,1]{1,2,0:T(1,128)S(1)}, s32[2,8,1]{1,2,0:T(1,128)}, u32[]{:S(2)}) copy-start(s32[2,8,1]{1,2,0:T(1,128)} %param.17) | copy-start | bytes 196
  9.1 15.0 %all-to-all-start = ((bf16[64,16,128]{2,0,1:T(8,128)(2,1)}), bf16[64,16,128]{2,0,1:T(8,128)(2,1)S(1)}, u32[]{:S(2)}, u32[]{:S(2)}) async-start(bf16[64,16,128]{2,0,1:T(8,128)(2,1)} %copy.56), calls=%async_computation | async-start | bytes 524288 | tf_op jit(solution)/shard_map/all_to_all | solution.py:93
  16.7 68.3 %all-gather.2.cloned.1.call-start = ((), (), s32[]{:S(2)}) async-start(), calls=%async_computation.9 | async-start | bytes 2228224 | tf_op jit(solution)/shard_map/all_gather | solution.py:127
  24.1 10.9 %all-to-all-start.1 = ((bf16[64,16,128]{2,0,1:T(8,128)(2,1)}), bf16[64,16,128]{2,0,1:T(8,128)(2,1)S(1)}, u32[]{:S(2)}, u32[]{:S(2)}) async-start(bf16[64,16,128]{2,0,1:T(8,128)(2,1)} %copy.57), calls=%async_computation.1 | async-start | bytes 524288 | tf_op jit(solution)/shard_map/all_to_all | solution.py:94
  35.1 10.8 %all-to-all-start.2 = ((bf16[64,16,128]{2,0,1:T(8,128)(2,1)}), bf16[64,16,128]{2,0,1:T(8,128)(2,1)S(1)}, u32[]{:S(2)}, u32[]{:S(2)}) async-start(bf16[64,16,128]{2,0,1:T(8,128)(2,1)} %copy.58), calls=%async_computation.2 | async-start | bytes 524288 | tf_op jit(solution)/shard_map/all_to_all | solution.py:95
  46.0 15.0 %copy-start.2 = (bf16[64,2,1024]{2,1,0:T(2,128)(2,1)S(1)}, bf16[64,2,1024]{2,1,0:T(2,128)(2,1)}, u32[]{:S(2)}) copy-start(bf16[64,2,1024]{2,1,0:T(2,128)(2,1)} %param.14) | copy-start | bytes 786436
  57.4 10.8 %all-to-all-start.3 = ((bf16[16,2,4096]{2,1,0:T(2,128)(2,1)}), bf16[16,2,4096]{2,1,0:T(2,128)(2,1)S(1)}, u32[]{:S(2)}, u32[]{:S(2)}) async-start(bf16[16,2,4096]{2,1,0:T(2,128)(2,1)} %reshape.209), calls=%async_computation.3 | async-start | bytes 524288 | tf_op jit(solution)/shard_map/all_to_all | solution.py:120
  60.9 122.8 %reduce-scatter.2.cloned.1.call-start = ((), (), s32[]{:S(2)}) async-start(), calls=%async_computation.10 | async-start | bytes 4456448 | tf_op jit(solution)/shard_map/reduce_scatter | solution.py:200
  88.3 12.0 %all-to-all-start.4 = ((bf16[64,16,128]{2,0,1:T(8,128)(2,1)}), bf16[64,16,128]{2,0,1:T(8,128)(2,1)S(1)}, u32[]{:S(2)}, u32[]{:S(2)}) async-start(bf16[64,16,128]{2,0,1:T(8,128)(2,1)} %copy.61), calls=%async_computation.4 | async-start | bytes 524288 | tf_op jit(solution)/shard_map/all_to_all | solution.py:134
  114.5 12.1 %all-to-all-start.5 = ((bf16[16,2,4096]{2,1,0:T(2,128)(2,1)}), bf16[16,2,4096]{2,1,0:T(2,128)(2,1)S(1)}, u32[]{:S(2)}, u32[]{:S(2)}) async-start(bf16[16,2,4096]{2,1,0:T(2,128)(2,1)} %reshape.211), calls=%async_computation.5 | async-start | bytes 524288 | tf_op jit(solution)/shard_map/all_to_all | solution.py:191
  118.2 70.2 %copy-start = (bf16[1024,1024]{1,0:T(8,128)(2,1)S(1)}, bf16[1024,1024]{1,0:T(8,128)(2,1)}, u32[]{:S(2)}) copy-start(bf16[1024,1024]{1,0:T(8,128)(2,1)} %all-gather.2.cloned.1.call-done) | copy-start | bytes 6291460
  126.5 57.2 %all-to-all-start.6 = ((bf16[16,2,4096]{2,1,0:T(2,128)(2,1)}), bf16[16,2,4096]{2,1,0:T(2,128)(2,1)S(1)}, u32[]{:S(2)}, u32[]{:S(2)}) async-start(bf16[16,2,4096]{2,1,0:T(2,128)(2,1)} %reshape.213), calls=%async_computation.6 | async-start | bytes 524288 | tf_op jit(solution)/shard_map/all_to_all | solution.py:192
  130.1 263.4 %all-reduce.2.cloned.1.call-start = ((), (), s32[]{:S(2)}) async-start(), calls=%async_computation.11 | async-start | bytes 524288 | tf_op jit(solution)/shard_map/psum | solution.py:209
  183.7 12.2 %all-to-all-start.7 = ((bf16[16,2,4096]{2,1,0:T(2,128)(2,1)}), bf16[16,2,4096]{2,1,0:T(2,128)(2,1)S(1)}, u32[]{:S(2)}, u32[]{:S(2)}) async-start(bf16[16,2,4096]{2,1,0:T(2,128)(2,1)} %reshape.215), calls=%async_computation.7 | async-start | bytes 524288 | tf_op jit(solution)/shard_map/all_to_all | solution.py:193
Sparse Core Ops, SparseCore 0:
  20.6 64.3 all-gather.1
  89.2 94.4 reduce-scatter.1
  186.1 207.3 all-reduce.1
where the time goes:
time: 403 us; the launch traced here: 402 us
  waiting for transfers between devices  304 us (75%)
  starting transfers between devices  35 us (9%)
  local copies, waits for them, and re-layouts  20 us (5%)
  matrix products  15.8 us (4%)
  between operations  14.1 us (3%)
  other arithmetic  9.88 us (2%)
    psum x1, waiting for transfers between devices, on_device(): weight_grad = lax.psum(partial_grad, 'dp')  196 us
    reduce_scatter x1, waiting for transfers between devices, on_device(): lax.psum_scatter(lax.dot_general(attended, flat_cot, (((0,), (0,)), ((),...  52 us
    all_gather x1, waiting for transfers between devices, on_device(): full_weight = lax.all_gather(out_weight, 'seq', axis=0, tiled=True)  13.2 us
  transfers between devices with their start and end apart: 11, of which 10 were waited for; matrix products, arithmetic and copies ran while one was open for 10% of the time, Pallas kernels for 0%

commit v1 on v0

v1 whole, which is shorter than its diff:
```python
import functools
import math

import jax
import jax.numpy as jnp
from jax import lax
from jax.experimental import pallas as pl
from jax.experimental.pallas import tpu as pltpu
from jax.sharding import PartitionSpec as P

HEAD = 128
BLOCK = 128
NODES = 1024
WIDTH = 1024
ROWS = 64
IB = 256
MESH = pl.DeviceIdType.MESH
BF = jnp.bfloat16
F32 = jnp.float32
NT = (((1,), (1,)), ((), ()))
MASKED = -1e30


def kernel(
    planes,
    q_ref,
    k_ref,
    v_ref,
    cot_ref,
    w_ref,
    count_ref,
    bits_ref,
    out_ref,
    dq_ref,
    dk_ref,
    dv_ref,
    wg_ref,
    qkv_s,
    cot_s,
    qkv_r,
    aux,
    cot_all,
    w_all,
    scores,
    prob,
    prob_b,
    sgrad,
    att_t,
    att_n,
    ag_n,
    ag_t,
    vt,
    kt,
    dqkv_n,
    att_ret,
    dqkv_ret,
    part,
    ry,
    zsrc,
    zr,
    zres,
    zag,
    ssem,
    rsem,
    cot_sem,
    w_sem,
    cot_ssem,
    w_ssem,
):
    dp = lax.axis_index("dp")
    seq = lax.axis_index("seq")
    z, c = dp // 2, dp % 2
    x, y = seq // 4, seq % 4
    head = 2 * x + c
    own_side = c == y // 2

    def dev(xd, yd, cd):
        return (2 * z + cd, 4 * xd + yd)

    sibling = dev(x, y, 1 - c)

    barrier = pltpu.get_barrier_semaphore()

    def greet(t, carry):
        other = lax.rem(seq + t, 16)
        pl.semaphore_signal(barrier, inc=1, device_id=(2 * z + 1 - c, other), device_id_type=MESH)

        @pl.when(t > 0)
        def _():
            pl.semaphore_signal(barrier, inc=1, device_id=(dp, other), device_id_type=MESH)

        return carry

    lax.fori_loop(0, 16, greet, 0)
    if planes > 1:

        def greet_z(t, carry):
            zd = lax.rem(z + t, planes)
            pl.semaphore_signal(barrier, inc=1, device_id=(2 * zd + c, seq), device_id_type=MESH)
            return carry

        lax.fori_loop(1, planes, greet_z, 0)

    qkv_s[0] = jnp.swapaxes(q_ref[...], 0, 1)
    qkv_s[1] = jnp.swapaxes(k_ref[...], 0, 1)
    qkv_s[2] = jnp.swapaxes(v_ref[...], 0, 1)
    cot_s[...] = jnp.swapaxes(cot_ref[...], 0, 1)

    @pl.when(own_side)
    def _():
        count = count_ref[y % 2]
        key_block = lax.broadcasted_iota(jnp.int32, (8, BLOCK), 0)
        lane = lax.broadcasted_iota(jnp.int32, (8, BLOCK), 1)
        for i in range(8):
            bits = bits_ref[y % 2, i]
            seen = (jnp.right_shift(jnp.full((8, BLOCK), bits, jnp.int32), key_block) & 1) == 1
            limit = jnp.where(seen, count - BLOCK * key_block, 0)
            aux[0:8, i * BLOCK : (i + 1) * BLOCK] = limit.astype(F32)
            live = lane + i * BLOCK < count
            aux[8:16, i * BLOCK : (i + 1) * BLOCK] = jnp.where(live, 1.0, 0.0)

    pl.semaphore_wait(barrier, 31 + planes - 1)

    def push(src, dst, to, s_sem, r_sem):
        same = (to[0] == dp) & (to[1] == seq)

        @pl.when(same)
        def _():
            pltpu.make_async_copy(src, dst, r_sem).start()

        @pl.when(jnp.logical_not(same))
        def _():
            pltpu.make_async_remote_copy(
                src, dst, s_sem, r_sem, device_id=to, device_id_type=MESH
            ).start()

    def send(src, dst, to, s_sem, r_sem):
        pltpu.make_async_remote_copy(
            src, dst, s_sem, r_sem, device_id=to, device_id_type=MESH
        ).start()

    def landed(ref, sem):
        pltpu.make_async_copy(ref, ref, sem).wait()

    @pl.when(own_side)
    def _():
        send(aux, aux, sibling, ssem.at[8], rsem.at[8])

    half = pl.ds(ROWS * (y % 2), ROWS)
    for j in range(2):
        to = dev(x, 2 * c + j, y // 2)
        push(cot_s.at[j], cot_all.at[2 * x + y // 2, half], to, ssem.at[0], rsem.at[0])
    for j in range(2):
        to = dev(x, 2 * c + j, y // 2)
        push(w_ref, w_all.at[2 * x + y // 2, half], to, ssem.at[1], rsem.at[1])

    def send_qkv(t, carry):
        xd = lax.rem(x + t // 4, 4)
        j = lax.rem(t // 2, 2)
        cd = lax.rem(t, 2)
        cols = pl.ds(pl.multiple_of(HEAD * (2 * xd + cd), HEAD), HEAD)
        push(
            qkv_s.at[:, j, :, cols],
            qkv_r.at[:, pl.ds(pl.multiple_of(ROWS * seq, ROWS), ROWS), :],
            dev(xd, 2 * c + j, cd),
            ssem.at[2],
            rsem.at[2],
        )
        return carry

    lax.fori_loop(0, 16, send_qkv, 0)

    right = dev(lax.rem(x + 1, 4), y, c)
    left = dev(lax.rem(x + 3, 4), y, c)
    b_own = head
    b_left = 2 * lax.rem(x + 3, 4) + c
    b_right = 2 * lax.rem(x + 1, 4) + c
    b_far = 2 * lax.rem(x + 2, 4) + c
    low, high = pl.ds(0, ROWS), pl.ds(ROWS, ROWS)

    def ring_first(buf, s, r):
        send(buf.at[b_own], buf.at[b_own], right, s.at[0], r.at[0])
        send(buf.at[b_own], buf.at[b_own], left, s.at[1], r.at[1])
        send(buf.at[b_own], buf.at[b_own], sibling, s.at[2], r.at[2])

    def ring_second(buf, s, r):
        landed(buf.at[b_left], r.at[0])
        send(buf.at[b_left, low], buf.at[b_left, low], right, s.at[4], r.at[4])
        landed(buf.at[b_right], r.at[1])
        send(buf.at[b_right, high], buf.at[b_right, high], left, s.at[6], r.at[6])
        send(buf.at[b_left], buf.at[b_left], sibling, s.at[3], r.at[3])
        send(buf.at[b_right], buf.at[b_right], sibling, s.at[5], r.at[5])

    def ring_third(buf, s, r):
        landed(buf.at[b_far, low], r.at[4])
        send(buf.at[b_far, low], buf.at[b_far, low], sibling, s.at[7], r.at[7])
        landed(buf.at[b_far, high], r.at[6])
        send(buf.at[b_far, high], buf.at[b_far, high], sibling, s.at[8], r.at[8])

    def ring_rest(buf, r):
        other = 1 - 2 * c
        landed(buf.at[b_own + other], r.at[2])
        landed(buf.at[b_left + other], r.at[3])
        landed(buf.at[b_right + other], r.at[5])
        landed(buf.at[b_far + other, low], r.at[7])
        landed(buf.at[b_far + other, high], r.at[8])

    def ring_drain(buf, s):
        for i in (0, 1, 2, 3, 5):
            landed(buf.at[0], s.at[i])
        for i in (4, 6, 7, 8):
            landed(buf.at[0, low], s.at[i])

    landed(cot_all.at[b_own], rsem.at[0])
    ring_first(cot_all, cot_ssem, cot_sem)

    @pl.when(jnp.logical_not(own_side))
    def _():
        landed(aux, rsem.at[8])

    landed(qkv_r, rsem.at[2])

    factor = math.log2(math.e) / math.sqrt(HEAD)
    key_pos = lax.broadcasted_iota(jnp.int32, (BLOCK, IB), 0).astype(F32)
    vt[...] = qkv_r[2].astype(F32).T.astype(BF)
    kt[...] = qkv_r[1].astype(F32).T.astype(BF)

    def forward(i, carry):
        at = pl.multiple_of(i * IB, IB)
        here = pl.ds(at, IB)
        q_part = qkv_r[0, here, :]
        top = jnp.full((8, IB), MASKED, F32)
        for b in range(8):
            rows = pl.ds(b * BLOCK, BLOCK)
            s = lax.dot_general(qkv_r[1, rows, :], q_part, NT, preferred_element_type=F32)
            s = jnp.where(key_pos < aux[b : b + 1, here], s * factor, MASKED)
            scores[rows, :] = s
            top = jnp.maximum(top, jnp.max(s.reshape(BLOCK // 8, 8, IB), axis=0))
        top = jnp.max(top, axis=0, keepdims=True)
        total = jnp.zeros((8, IB), F32)
        for b in range(8):
            rows = pl.ds(b * BLOCK, BLOCK)
            e = jnp.exp2(scores[rows, :] - top)
            scores[rows, :] = e
            total = total + jnp.sum(e.reshape(BLOCK // 8, 8, IB), axis=0)
        inverse = 1.0 / jnp.sum(total, axis=0, keepdims=True)
        for b in range(8):
            rows = pl.ds(b * BLOCK, BLOCK)
            p = scores[rows, :] * inverse
            prob[i, rows, :] = p
            prob_b[rows, here] = p.astype(BF)
        mixed = jnp.dot(vt[...], prob_b[:, here], preferred_element_type=F32)
        mixed = jnp.where(aux[8:9, here] > 0.5, mixed, 0.0)
        att_t[:, here] = mixed.astype(BF)
        att_n[here, :] = mixed.T.astype(BF)
        return carry

    lax.fori_loop(0, 2, forward, 0)
    ring_second(cot_all, cot_ssem, cot_sem)
    landed(w_all.at[b_own], rsem.at[1])
    lax.fori_loop(2, 4, forward, 0)

    my_cols = pl.ds(pl.multiple_of(HEAD * head, HEAD), HEAD)

    def give_back(src, dst, s_sem, r_sem, first, count):
        def one(t, carry):
            to = first + t if count < 16 else lax.rem(seq + t, 16)
            push(
                src.at[pl.ds(pl.multiple_of(ROWS * to, ROWS), ROWS), :],
                dst.at[y % 2, :, my_cols],
                (2 * z + y // 2, to),
                s_sem,
                r_sem,
            )
            return carry

        lax.fori_loop(0, count, one, 0)

    give_back(att_n, att_ret, ssem.at[3], rsem.at[3], 0, 16)

    ring_third(cot_all, cot_ssem, cot_sem)
    ring_rest(cot_all, cot_sem)
    ring_first(w_all, w_ssem, w_sem)

    for b in range(8):
        rows = pl.ds(b * BLOCK, BLOCK)
        g = lax.dot_general(cot_all[b], w_all[b_own], NT, preferred_element_type=F32)
        gt = jnp.where(aux[8:9, b * BLOCK : (b + 1) * BLOCK] > 0.5, g.T, 0.0)
        ag_t[:, rows] = gt.astype(BF)
        ag_n[rows, :] = gt.T.astype(BF)
    part[...] = jnp.dot(
        att_t[...], cot_all[...].reshape(NODES, WIDTH), preferred_element_type=F32
    ).astype(BF)
    for r in range(2):
        for cd in range(2):
            push(
                part.at[pl.ds(ROWS * r, ROWS), pl.ds(512 * cd, 512)],
                ry.at[y],
                dev(x, 2 * c + r, cd),
                ssem.at[7],
                rsem.at[7],
            )

    dqkv_n[2] = jnp.dot(prob_b[...], ag_n[...], preferred_element_type=F32).astype(BF)
    give_back(dqkv_n.at[2], dqkv_ret.at[2], ssem.at[6], rsem.at[6], 0, 16)

    ring_second(w_all, w_ssem, w_sem)

    scale = 1.0 / math.sqrt(HEAD)

    def backward(step, carry):
        i = lax.rem(x + step, 4)
        at = pl.multiple_of(i * IB, IB)
        here = pl.ds(at, IB)
        g_part = ag_n[here, :]
        centre = jnp.sum(
            ag_t[:, here].astype(F32) * att_t[:, here].astype(F32), axis=0, keepdims=True
        )
        for b in range(8):
            rows = pl.ds(b * BLOCK, BLOCK)
            pg = lax.dot_general(qkv_r[2, rows, :], g_part, NT, preferred_element_type=F32)
            sgrad[rows, here] = (prob[i, rows, :] * ((pg - centre) * scale)).astype(BF)
        dq = jnp.dot(kt[...], sgrad[:, here], preferred_element_type=F32)
        dqkv_n[0, here, :] = dq.T.astype(BF)
        give_back(dqkv_n.at[0], dqkv_ret.at[0], ssem.at[4], rsem.at[4], 4 * i, 4)
        return carry

    lax.fori_loop(0, 2, backward, 0)

    landed(ry, rsem.at[7])
    total = ry[0].astype(F32) + ry[1].astype(F32) + ry[2].astype(F32) + ry[3].astype(F32)
    zsrc[...] = total.astype(BF)

    def corner(p, left_edge=0):
        return (
            pl.ds(pl.multiple_of(16 * (p // 4), 16), 16),
            pl.ds(pl.multiple_of(left_edge + 128 * lax.rem(p, 4), 128), 128),
        )

    if planes > 1:

        def send_z(t, carry):
            zd = lax.rem(z + t, planes)
            rows, cols = corner(zd)
            push(
                zsrc.at[rows, cols], zr.at[z], (2 * zd + c, seq), ssem.at[9], rsem.at[9]
            )
            return carry

        lax.fori_loop(0, planes, send_z, 0)

    lax.fori_loop(2, 4, backward, 0)

    dqkv_n[1] = jnp.dot(sgrad[...], qkv_r[0], preferred_element_type=F32).astype(BF)
    give_back(dqkv_n.at[1], dqkv_ret.at[1], ssem.at[5], rsem.at[5], 0, 16)

    my_half = pl.ds(pl.multiple_of(512 * c, 512), 512)
    if planes > 1:
        landed(zr, rsem.at[9])
        zsum = zr[0].astype(F32)
        for p in range(1, planes):
            zsum = zsum + zr[p].astype(F32)
        zres[...] = (zsum * (1.0 / 256.0)).astype(BF)

        def spread(t, carry):
            zd = lax.rem(z + t, planes)
            rows, cols = corner(z, 512 * c)
            push(zres, zag.at[rows, cols], (2 * zd + c, seq), ssem.at[10], rsem.at[10])
            return carry

        lax.fori_loop(0, planes, spread, 0)
    else:
        zag[:, my_half] = (total * (1.0 / 256.0)).astype(BF)

    ring_third(w_all, w_ssem, w_sem)
    landed(att_ret, rsem.at[3])
    ring_rest(w_all, w_sem)
    done = jnp.dot(
        att_ret[...].reshape(2 * ROWS, WIDTH),
        w_all[...].reshape(WIDTH, WIDTH),
        preferred_element_type=F32,
    ).astype(BF)
    done = done.reshape(2, ROWS, WIDTH)
    out_ref[:, 0, :] = done[0]
    out_ref[:, 1, :] = done[1]

    if planes > 1:
        landed(zag.at[:, my_half], rsem.at[10])
    send(zag.at[:, my_half], zag.at[:, my_half], sibling, ssem.at[11], rsem.at[11])

    for i, ref in ((2, dv_ref), (0, dq_ref), (1, dk_ref)):
        landed(dqkv_ret.at[i], rsem.at[4 + i])
        ref[:, 0, :] = dqkv_ret[i, 0]
        ref[:, 1, :] = dqkv_ret[i, 1]

    landed(zag.at[:, pl.ds(pl.multiple_of(512 - 512 * c, 512), 512)], rsem.at[11])
    wg_ref[...] = zag[...].astype(F32)

    def left_here(sem, whole, short, is_short):
        @pl.when(is_short)
        def _():
            landed(short, sem)

        @pl.when(jnp.logical_not(is_short))
        def _():
            landed(whole, sem)

    @pl.when(own_side)
    def _():
        landed(aux, ssem.at[8])

    left_here(ssem.at[0], cot_s, cot_s.at[0], own_side)
    left_here(ssem.at[1], cot_s, cot_s.at[0], own_side)
    most = pl.ds(0, 15 * ROWS)
    left_here(ssem.at[2], qkv_r, qkv_r.at[:, most], own_side)
    left_here(ssem.at[3], att_n, att_n.at[most], own_side)
    for i in range(3):
        left_here(ssem.at[4 + i], dqkv_n.at[i], dqkv_n.at[i, most], own_side)
    left_here(ssem.at[7], ry, ry.at[pl.ds(0, 3)], own_side)
    if planes > 1:
        landed(zr.at[pl.ds(0, planes - 1)], ssem.at[9])
        landed(zr.at[pl.ds(0, planes - 1)], ssem.at[10])
    landed(zag.at[:, my_half], ssem.at[11])
    ring_drain(cot_all, cot_ssem)
    ring_drain(w_all, w_ssem)


def on_device(queries, key_rows, value_rows, cotangent, out_weight, node_counts, edge_bits):
    planes = lax.axis_size("dp") // 2
    vmem = pl.BlockSpec(memory_space=pltpu.VMEM)
    smem = pl.BlockSpec(memory_space=pltpu.SMEM)
    rows3 = jax.ShapeDtypeStruct((ROWS, 2, WIDTH), BF)
    dma = pltpu.SemaphoreType.DMA
    return pl.pallas_call(
        functools.partial(kernel, planes),
        out_shape=(rows3, rows3, rows3, rows3, jax.ShapeDtypeStruct((ROWS, WIDTH), F32)),
        in_specs=[vmem] * 5 + [smem] * 2,
        out_specs=(vmem,) * 5,
        scratch_shapes=[
            pltpu.VMEM((3, 2, ROWS, WIDTH), BF),
            pltpu.VMEM((2, ROWS, WIDTH), BF),
            pltpu.VMEM((3, NODES, HEAD), BF),
            pltpu.VMEM((16, NODES), F32),
            pltpu.VMEM((8, BLOCK, WIDTH), BF),
            pltpu.VMEM((8, BLOCK, WIDTH), BF),
            pltpu.VMEM((NODES, IB), F32),
            pltpu.VMEM((NODES // IB, NODES, IB), F32),
            pltpu.VMEM((NODES, NODES), BF),
            pltpu.VMEM((NODES, NODES), BF),
            pltpu.VMEM((HEAD, NODES), BF),
            pltpu.VMEM((NODES, HEAD), BF),
            pltpu.VMEM((NODES, HEAD), BF),
            pltpu.VMEM((HEAD, NODES), BF),
            pltpu.VMEM((HEAD, NODES), BF),
            pltpu.VMEM((HEAD, NODES), BF),
            pltpu.VMEM((3, NODES, HEAD), BF),
            pltpu.VMEM((2, ROWS, WIDTH), BF),
            pltpu.VMEM((3, 2, ROWS, WIDTH), BF),
            pltpu.VMEM((HEAD, WIDTH), BF),
            pltpu.VMEM((4, ROWS, 512), BF),
            pltpu.VMEM((ROWS, 512), BF),
            pltpu.VMEM((16, 16, 128), BF),
            pltpu.VMEM((16, 128), BF),
            pltpu.VMEM((ROWS, WIDTH), BF),
            dma((12,)),
            dma((12,)),
            dma((9,)),
            dma((9,)),
            dma((9,)),
            dma((9,)),
        ],
        compiler_params=pltpu.CompilerParams(
            collective_id=0, has_side_effects=True, vmem_limit_bytes=48 * 1024 * 1024
        ),
        cost_estimate=pl.CostEstimate(
            flops=3_000_000_000, bytes_accessed=3_000_000, transcendentals=1_000_000
        ),
        name="sublayer",
    )(
        queries,
        key_rows,
        value_rows,
        cotangent,
        out_weight,
        node_counts,
        edge_bits.reshape(2, 8),
    )


def solution(mesh):
    rows = P("seq", "dp", None)
    weight = P("seq", None)
    return jax.shard_map(
        on_device,
        mesh=mesh,
        in_specs=(rows, rows, rows, rows, weight, P("dp"), P("dp", None, None)),
        out_specs=(rows, rows, rows, rows, weight),
        check_vma=False,
    )
```

time: 403 us -> 87.9 us (0.22)
  waiting for transfers between devices: 304 us -> 0 us
  Pallas kernels: 0 us -> 78.1 us
  starting transfers between devices: 35 us -> 0 us
  matrix products: 15.8 us -> 0 us
  between operations: 14.1 us -> 0.67 us
  local copies, waits for them, and re-layouts: 20 us -> 8.88 us
  other arithmetic: 9.88 us -> 0 us
    psum x1 -> x0, waiting for transfers between devices: 196 us -> none  [on_device(): weight_grad = lax.psum(partial_grad, 'dp')]
    pallas_call x0 -> x1, Pallas kernels: none -> 78.1 us  [on_device(): pl.pallas_call(functools.partial(kernel, planes), out_shape=(rows3, rows3...]
    reduce_scatter x1 -> x0, waiting for transfers between devices: 52 us -> none  [on_device(): lax.psum_scatter(lax.dot_general(attended, flat_cot, (((0,), (0,)), ((),...]
    all_to_all x8 -> x0, waiting for transfers between devices: 41.9 us -> none  [the longest x1 7.3 us: on_device(): lax.all_to_all(att_grad.reshape(node_rows, item_count, head_size), 'seq',...]
    all_to_all x8 -> x0, starting transfers between devices: 34.9 us -> none  [the longest x1 7.58 us: on_device(): lax.all_to_all(split_heads(queries), 'seq', split_axis=1, concat_axis=0,...]
    dot_general x17 -> x0, matrix products: 15.8 us -> none  [the longest x4 3.61 us: probabilities(): lax.dot_general(query_part, key_all, (((1,), (1,)), ((), ())), preferred_...]
    all_gather x1 -> x0, waiting for transfers between devices: 13.2 us -> none  [on_device(): full_weight = lax.all_gather(out_weight, 'seq', axis=0, tiled=True)]
    reshape x15 -> x0, local copies, waits for them, and re-layouts: 9.06 us -> none  [the longest x6 4.77 us: split_heads(): return values_in.reshape(node_rows, item_count, head_size)]
  transfers between devices with their start and end apart: 11 -> 0, of which waited for: 10 -> 0; matrix products, arithmetic and copies ran while one was open for 10% -> 0% of each run, Pallas kernels for 0% -> 0%
where the time goes in v1:
time: 87.9 us; the launch traced here: 87.6 us
  Pallas kernels  78.1 us (89%)
  local copies, waits for them, and re-layouts  8.88 us (10%)
    pallas_call x1, Pallas kernels, on_device(): pl.pallas_call(functools.partial(kernel, planes), out_shape=(rows3, rows3...  78.1 us
    unnamed x19, local copies, waits for them, and re-layouts  8.88 us

profile of v1, /device:TPU:1, one launch (start us, length us, event | category | flops | bytes accessed | tf_op | source)
XLA Modules:
  0.0 87.6 jit_solution(4927674681442958371)
XLA Ops:
  0.6 0.0 copy-start.5
  0.6 0.0 copy-start.6
  0.7 0.7 copy-done.5
  1.3 0.0 copy-done.6
  1.3 0.0 copy-start
  1.3 0.9 %copy-done = bf16[64,2,1024]{2,1,0:T(2,128)(2,1)S(1)} copy-done((bf16[64,2,1024]{2,1,0:T(2,128)(2,1)S(1)}, bf16[64,2,1024]{2,1,0:T(2,128)(2,1)}, u32[]{:S(2)}) %copy-start) | copy-done | bytes 262168
  2.3 0.0 copy-start.1
  2.3 0.9 %copy-done.1 = bf16[64,2,1024]{2,1,0:T(2,128)(2,1)S(1)} copy-done((bf16[64,2,1024]{2,1,0:T(2,128)(2,1)S(1)}, bf16[64,2,1024]{2,1,0:T(2,128)(2,1)}, u32[]{:S(2)}) %copy-start.1) | copy-done | bytes 262168
  3.2 0.0 copy-start.2
  3.2 0.9 %copy-done.2 = bf16[64,2,1024]{2,1,0:T(2,128)(2,1)S(1)} copy-done((bf16[64,2,1024]{2,1,0:T(2,128)(2,1)S(1)}, bf16[64,2,1024]{2,1,0:T(2,128)(2,1)}, u32[]{:S(2)}) %copy-start.2) | copy-done | bytes 262168
  4.2 0.0 copy-start.3
  4.2 0.9 %copy-done.3 = bf16[64,2,1024]{2,1,0:T(2,128)(2,1)S(1)} copy-done((bf16[64,2,1024]{2,1,0:T(2,128)(2,1)S(1)}, bf16[64,2,1024]{2,1,0:T(2,128)(2,1)}, u32[]{:S(2)}) %copy-start.3) | copy-done | bytes 262168
  5.1 0.0 copy-start.4
  5.1 0.9 %copy-done.4 = bf16[64,1024]{1,0:T(8,128)(2,1)S(1)} copy-done((bf16[64,1024]{1,0:T(8,128)(2,1)S(1)}, bf16[64,1024]{1,0:T(8,128)(2,1)}, u32[]{:S(2)}) %copy-start.4) | copy-done | bytes 131096
  6.0 78.1 %sublayer.1 = (bf16[64,2,1024]{2,1,0:T(2,128)(2,1)S(1)}, bf16[64,2,1024]{2,1,0:T(2,128)(2,1)S(1)}, bf16[64,2,1024]{2,1,0:T(2,128)(2,1)S(1)}, bf16[64,2,1024]{2,1,0:T(2,128)(2,1)S(1)}, f32[64,1024]{1,0:T(8,128)S(1)}) custom-call(bf16[64,2,1024]{2,1,0:T(2,128)(2,1)S(1)} %copy-done, bf16[64,2,1024]{2,1,0:T(2,128)(2,1)S(1)} %copy-done.1, ...), custom_call_target="tpu_custom_call" | custom-call | flops 3000000000 | bytes 3000000 | tf_op jit(solution)/shard_map/sublayer/pallas_call | solution.py:434
  84.1 0.7 copy.17
  84.8 0.7 copy.18
  85.5 0.7 copy.19
  86.2 0.7 copy.20
  86.9 0.7 copy.21
Async XLA Ops:
  0.6 0.7 copy-start.5
  0.6 0.7 copy-start.6
  1.3 1.0 %copy-start = (bf16[64,2,1024]{2,1,0:T(2,128)(2,1)S(1)}, bf16[64,2,1024]{2,1,0:T(2,128)(2,1)}, u32[]{:S(2)}) copy-start(bf16[64,2,1024]{2,1,0:T(2,128)(2,1)} %q_ref.1) | copy-start | bytes 786436
  2.3 0.9 %copy-start.1 = (bf16[64,2,1024]{2,1,0:T(2,128)(2,1)S(1)}, bf16[64,2,1024]{2,1,0:T(2,128)(2,1)}, u32[]{:S(2)}) copy-start(bf16[64,2,1024]{2,1,0:T(2,128)(2,1)} %k_ref.1) | copy-start | bytes 786436
  3.2 0.9 %copy-start.2 = (bf16[64,2,1024]{2,1,0:T(2,128)(2,1)S(1)}, bf16[64,2,1024]{2,1,0:T(2,128)(2,1)}, u32[]{:S(2)}) copy-start(bf16[64,2,1024]{2,1,0:T(2,128)(2,1)} %v_ref.1) | copy-start | bytes 786436
  4.2 0.9 %copy-start.3 = (bf16[64,2,1024]{2,1,0:T(2,128)(2,1)S(1)}, bf16[64,2,1024]{2,1,0:T(2,128)(2,1)}, u32[]{:S(2)}) copy-start(bf16[64,2,1024]{2,1,0:T(2,128)(2,1)} %cot_ref.1) | copy-start | bytes 786436
  5.1 0.9 %copy-start.4 = (bf16[64,1024]{1,0:T(8,128)(2,1)S(1)}, bf16[64,1024]{1,0:T(8,128)(2,1)}, u32[]{:S(2)}) copy-start(bf16[64,1024]{1,0:T(8,128)(2,1)} %w_ref.1) | copy-start | bytes 393220

commit v2 on v1

v2 whole, which is shorter than its diff:
```python
import functools
import math

import jax
import jax.numpy as jnp
from jax import lax
from jax.experimental import pallas as pl
from jax.experimental.pallas import tpu as pltpu
from jax.sharding import PartitionSpec as P

HEAD = 128
BLOCK = 128
NODES = 1024
WIDTH = 1024
ROWS = 64
IB = 256
MESH = pl.DeviceIdType.MESH
BF = jnp.bfloat16
F32 = jnp.float32
NT = (((1,), (1,)), ((), ()))
MASKED = -1e30


def kernel(
    planes,
    q_ref,
    k_ref,
    v_ref,
    cot_ref,
    w_hbm,
    count_hbm,
    bits_hbm,
    out_ref,
    dq_ref,
    dk_ref,
    dv_ref,
    grad_ref,
    raw,
    w_ref,
    count_ref,
    bits_ref,
    qkv_s,
    cot_s,
    qkv_r,
    aux,
    cot_all,
    w_all,
    scores,
    prob,
    prob_b,
    sgrad,
    att_t,
    att_n,
    ag_n,
    ag_t,
    vt,
    kt,
    dqkv_n,
    att_ret,
    dqkv_ret,
    part,
    ry,
    zsrc,
    zr,
    zres,
    zag,
    mixed_rows,
    wg_f32,
    in_sem,
    out_sem,
    ssem,
    rsem,
    cot_sem,
    w_sem,
    cot_ssem,
    w_ssem,
):
    dp = lax.axis_index("dp")
    seq = lax.axis_index("seq")
    z, c = dp // 2, dp % 2
    x, y = seq // 4, seq % 4
    head = 2 * x + c
    own_side = c == y // 2

    def dev(xd, yd, cd):
        return (2 * z + cd, 4 * xd + yd)

    sibling = dev(x, y, 1 - c)

    incoming = [
        pltpu.make_async_copy(src, dst, in_sem.at[i])
        for i, (src, dst) in enumerate(
            (
                (cot_ref, raw.at[3]),
                (q_ref, raw.at[0]),
                (k_ref, raw.at[1]),
                (v_ref, raw.at[2]),
                (w_hbm, w_ref),
                (count_hbm, count_ref),
                (bits_hbm, bits_ref),
            )
        )
    ]
    for copy in incoming:
        copy.start()

    barrier = pltpu.get_barrier_semaphore()

    def greet(to):
        pl.semaphore_signal(barrier, inc=1, device_id=to, device_id_type=MESH)

    def greet_plane(t, carry):
        xd, j, cd = lax.rem(x + t // 4 + 2, 4), lax.rem(t // 2, 2), lax.rem(t, 2)
        to = dev(xd, 2 * c + j, cd)

        @pl.when(jnp.logical_not((to[0] == dp) & (to[1] == seq)))
        def _():
            greet(to)

        @pl.when(cd == 0)
        def _():
            greet(dev(xd, 2 * (1 - c) + j, y // 2))

        return carry

    def greet_z(t, carry):
        zd = lax.rem(z + t, planes)
        greet((2 * zd, seq))
        greet((2 * zd + 1, seq))
        return carry

    if planes > 1:
        lax.fori_loop(1, planes, greet_z, 0)
    lax.fori_loop(0, 16, greet_plane, 0)

    @pl.when(jnp.logical_not(own_side))
    def _():
        greet(dev(lax.rem(x + 1, 4), y, c))
        greet(dev(lax.rem(x + 3, 4), y, c))

    incoming[0].wait()
    cot_s[...] = jnp.swapaxes(raw[3], 0, 1)
    for i in range(3):
        incoming[1 + i].wait()
        qkv_s[i] = jnp.swapaxes(raw[i], 0, 1)

    @pl.when(own_side)
    def _():
        pl.semaphore_wait(barrier, 23 + 2 * (planes - 1))

    @pl.when(jnp.logical_not(own_side))
    def _():
        pl.semaphore_wait(barrier, 26 + 2 * (planes - 1))

    def push(src, dst, to, s_sem, r_sem):
        same = (to[0] == dp) & (to[1] == seq)

        @pl.when(same)
        def _():
            pltpu.make_async_copy(src, dst, r_sem).start()

        @pl.when(jnp.logical_not(same))
        def _():
            pltpu.make_async_remote_copy(
                src, dst, s_sem, r_sem, device_id=to, device_id_type=MESH
            ).start()

    def send(src, dst, to, s_sem, r_sem):
        pltpu.make_async_remote_copy(
            src, dst, s_sem, r_sem, device_id=to, device_id_type=MESH
        ).start()

    def landed(ref, sem):
        pltpu.make_async_copy(ref, ref, sem).wait()

    half = pl.ds(ROWS * (y % 2), ROWS)
    for j in range(2):
        to = dev(x, 2 * c + j, y // 2)
        push(cot_s.at[j], cot_all.at[2 * x + y // 2, half], to, ssem.at[0], rsem.at[12 + y % 2])

    def send_qkv(first, count, sem):
        def one(t, carry):
            xd, j, cd = lax.rem(x + t // 4 + 2, 4), lax.rem(t // 2, 2), lax.rem(t, 2)
            cols = pl.ds(pl.multiple_of(HEAD * (2 * xd + cd), HEAD), HEAD)
            push(
                qkv_s.at[pl.ds(first, count), j, :, cols],
                qkv_r.at[pl.ds(first, count), pl.ds(pl.multiple_of(ROWS * seq, ROWS), ROWS), :],
                dev(xd, 2 * c + j, cd),
                ssem.at[sem],
                rsem.at[sem],
            )
            return carry

        lax.fori_loop(0, 16, one, 0)

    send_qkv(0, 2, 2)
    send_qkv(2, 1, 9)

    incoming[5].wait()
    incoming[6].wait()

    @pl.when(own_side)
    def _():
        count = count_ref[y % 2]
        key_block = lax.broadcasted_iota(jnp.int32, (8, BLOCK), 0)
        lane = lax.broadcasted_iota(jnp.int32, (8, BLOCK), 1)
        for i in range(8):
            bits = bits_ref[y % 2, i]
            seen = (jnp.right_shift(jnp.full((8, BLOCK), bits, jnp.int32), key_block) & 1) == 1
            limit = jnp.where(seen, count - BLOCK * key_block, 0)
            aux[0:8, i * BLOCK : (i + 1) * BLOCK] = limit.astype(F32)
            live = lane + i * BLOCK < count
            aux[8:16, i * BLOCK : (i + 1) * BLOCK] = jnp.where(live, 1.0, 0.0)
        send(aux, aux, sibling, ssem.at[8], rsem.at[8])

    right = dev(lax.rem(x + 1, 4), y, c)
    left = dev(lax.rem(x + 3, 4), y, c)
    b_own = head
    b_left = 2 * lax.rem(x + 3, 4) + c
    b_right = 2 * lax.rem(x + 1, 4) + c
    b_far = 2 * lax.rem(x + 2, 4) + c
    low, high = pl.ds(0, ROWS), pl.ds(ROWS, ROWS)

    def ring_own(buf, s, r):
        for i, rows, to in (
            (0, low, right),
            (2, high, left),
            (1, high, right),
            (3, low, left),
            (6, low, sibling),
            (7, high, sibling),
        ):
            send(buf.at[b_own, rows], buf.at[b_own, rows], to, s.at[i], r.at[i])

    def ring_forward(buf, s, r):
        landed(buf.at[b_left, low], r.at[0])
        send(buf.at[b_left, low], buf.at[b_left, low], right, s.at[4], r.at[4])
        landed(buf.at[b_right, high], r.at[2])
        send(buf.at[b_right, high], buf.at[b_right, high], left, s.at[5], r.at[5])

    def ring_relay(buf, s, r):
        send(buf.at[b_left, low], buf.at[b_left, low], sibling, s.at[8], r.at[8])
        send(buf.at[b_right, high], buf.at[b_right, high], sibling, s.at[10], r.at[10])
        landed(buf.at[b_left, high], r.at[1])
        send(buf.at[b_left, high], buf.at[b_left, high], sibling, s.at[9], r.at[9])
        landed(buf.at[b_right, low], r.at[3])
        send(buf.at[b_right, low], buf.at[b_right, low], sibling, s.at[11], r.at[11])

    def ring_far(buf, s, r):
        landed(buf.at[b_far, low], r.at[4])
        send(buf.at[b_far, low], buf.at[b_far, low], sibling, s.at[12], r.at[12])
        landed(buf.at[b_far, high], r.at[5])
        send(buf.at[b_far, high], buf.at[b_far, high], sibling, s.at[13], r.at[13])

    def ring_rest(buf, r):
        other = 1 - 2 * c
        for i, b, rows in (
            (6, b_own, low),
            (7, b_own, high),
            (8, b_left, low),
            (9, b_left, high),
            (10, b_right, high),
            (11, b_right, low),
            (12, b_far, low),
            (13, b_far, high),
        ):
            landed(buf.at[b + other, rows], r.at[i])

    def ring_drain(buf, s):
        for i in range(14):
            landed(buf.at[0, low], s.at[i])

    landed(cot_all.at[b_own, low], rsem.at[12])
    landed(cot_all.at[b_own, high], rsem.at[13])
    ring_own(cot_all, cot_ssem, cot_sem)
    ring_forward(cot_all, cot_ssem, cot_sem)

    @pl.when(jnp.logical_not(own_side))
    def _():
        landed(aux, rsem.at[8])

    landed(qkv_r.at[pl.ds(0, 2)], rsem.at[2])

    incoming[4].wait()
    for j in range(2):
        to = dev(x, 2 * c + j, y // 2)
        push(w_ref, w_all.at[2 * x + y // 2, half], to, ssem.at[1], rsem.at[14 + y % 2])

    factor = math.log2(math.e) / math.sqrt(HEAD)
    key_pos = lax.broadcasted_iota(jnp.int32, (BLOCK, IB), 0).astype(F32)

    def forward(i, carry):
        at = pl.multiple_of(i * IB, IB)
        here = pl.ds(at, IB)
        q_part = qkv_r[0, here, :]
        top = jnp.full((8, IB), MASKED, F32)
        for b in range(8):
            rows = pl.ds(b * BLOCK, BLOCK)
            s = lax.dot_general(qkv_r[1, rows, :], q_part, NT, preferred_element_type=F32)
            s = jnp.where(key_pos < aux[b : b + 1, here], s * factor, MASKED)
            scores[rows, :] = s
            top = jnp.maximum(top, jnp.max(s.reshape(BLOCK // 8, 8, IB), axis=0))
        top = jnp.max(top, axis=0, keepdims=True)
        total = jnp.zeros((8, IB), F32)
        for b in range(8):
            rows = pl.ds(b * BLOCK, BLOCK)
            e = jnp.exp2(scores[rows, :] - top)
            scores[rows, :] = e
            total = total + jnp.sum(e.reshape(BLOCK // 8, 8, IB), axis=0)
        inverse = 1.0 / jnp.sum(total, axis=0, keepdims=True)
        for b in range(8):
            rows = pl.ds(b * BLOCK, BLOCK)
            p = scores[rows, :] * inverse
            prob[i, rows, :] = p
            prob_b[rows, here] = p.astype(BF)
        return carry

    lax.fori_loop(0, 4, forward, 0)
    ring_relay(cot_all, cot_ssem, cot_sem)
    kt[...] = qkv_r[1].astype(F32).T.astype(BF)
    landed(qkv_r.at[pl.ds(2, 1)], rsem.at[9])
    vt[...] = qkv_r[2].astype(F32).T.astype(BF)

    def mix(i, carry):
        here = pl.ds(pl.multiple_of(i * IB, IB), IB)
        mixed = jnp.dot(vt[...], prob_b[:, here], preferred_element_type=F32)
        mixed = jnp.where(aux[8:9, here] > 0.5, mixed, 0.0)
        att_t[:, here] = mixed.astype(BF)
        att_n[here, :] = mixed.T.astype(BF)
        return carry

    lax.fori_loop(0, 4, mix, 0)

    my_cols = pl.ds(pl.multiple_of(HEAD * head, HEAD), HEAD)

    def give_back(src, dst, s_sem, r_sem, first, count):
        def one(t, carry):
            to = first + t if count < 16 else lax.rem(seq + t, 16)
            push(
                src.at[pl.ds(pl.multiple_of(ROWS * to, ROWS), ROWS), :],
                dst.at[y % 2, :, my_cols],
                (2 * z + y // 2, to),
                s_sem,
                r_sem,
            )
            return carry

        lax.fori_loop(0, count, one, 0)

    ring_far(cot_all, cot_ssem, cot_sem)
    give_back(att_n, att_ret, ssem.at[3], rsem.at[3], 0, 16)
    ring_rest(cot_all, cot_sem)

    part[...] = jnp.dot(
        att_t[...], cot_all[...].reshape(NODES, WIDTH), preferred_element_type=F32
    ).astype(BF)
    for r in range(2):
        for cd in range(2):
            push(
                part.at[pl.ds(ROWS * r, ROWS), pl.ds(512 * cd, 512)],
                ry.at[y],
                dev(x, 2 * c + r, cd),
                ssem.at[7],
                rsem.at[7],
            )
    landed(w_all.at[b_own, low], rsem.at[14])
    landed(w_all.at[b_own, high], rsem.at[15])
    for b in range(8):
        rows = pl.ds(b * BLOCK, BLOCK)
        g = lax.dot_general(cot_all[b], w_all[b_own], NT, preferred_element_type=F32)
        gt = jnp.where(aux[8:9, b * BLOCK : (b + 1) * BLOCK] > 0.5, g.T, 0.0)
        ag_t[:, rows] = gt.astype(BF)
        ag_n[rows, :] = gt.T.astype(BF)

    dqkv_n[2] = jnp.dot(prob_b[...], ag_n[...], preferred_element_type=F32).astype(BF)
    give_back(dqkv_n.at[2], dqkv_ret.at[2], ssem.at[6], rsem.at[6], 0, 16)

    scale = 1.0 / math.sqrt(HEAD)

    def backward(step, carry):
        i = lax.rem(x + step, 4)
        at = pl.multiple_of(i * IB, IB)
        here = pl.ds(at, IB)
        g_part = ag_n[here, :]
        centre = jnp.sum(
            ag_t[:, here].astype(F32) * att_t[:, here].astype(F32), axis=0, keepdims=True
        )
        for b in range(8):
            rows = pl.ds(b * BLOCK, BLOCK)
            pg = lax.dot_general(qkv_r[2, rows, :], g_part, NT, preferred_element_type=F32)
            sgrad[rows, here] = (prob[i, rows, :] * ((pg - centre) * scale)).astype(BF)
        dq = jnp.dot(kt[...], sgrad[:, here], preferred_element_type=F32)
        dqkv_n[0, here, :] = dq.T.astype(BF)
        give_back(dqkv_n.at[0], dqkv_ret.at[0], ssem.at[4], rsem.at[4], 4 * i, 4)
        return carry

    lax.fori_loop(0, 2, backward, 0)

    landed(ry, rsem.at[7])
    total = ry[0].astype(F32) + ry[1].astype(F32) + ry[2].astype(F32) + ry[3].astype(F32)
    zsrc[...] = total.astype(BF)

    def corner(p, left_edge=0):
        return (
            pl.ds(pl.multiple_of(16 * (p // 4), 16), 16),
            pl.ds(pl.multiple_of(left_edge + 128 * lax.rem(p, 4), 128), 128),
        )

    if planes > 1:

        def send_z(t, carry):
            zd = lax.rem(z + t + planes // 2, planes)
            rows, cols = corner(zd)
            push(zsrc.at[rows, cols], zr.at[z], (2 * zd + c, seq), ssem.at[10], rsem.at[10])
            return carry

        lax.fori_loop(0, planes, send_z, 0)

    lax.fori_loop(2, 4, backward, 0)

    dqkv_n[1] = jnp.dot(sgrad[...], qkv_r[0], preferred_element_type=F32).astype(BF)
    give_back(dqkv_n.at[1], dqkv_ret.at[1], ssem.at[5], rsem.at[5], 0, 16)
    ring_own(w_all, w_ssem, w_sem)

    my_half = pl.ds(pl.multiple_of(512 * c, 512), 512)
    if planes > 1:
        landed(zr, rsem.at[10])
        zsum = zr[0].astype(F32)
        for p in range(1, planes):
            zsum = zsum + zr[p].astype(F32)
        zres[...] = (zsum * (1.0 / 256.0)).astype(BF)

        def spread(t, carry):
            zd = lax.rem(z + t // 2 + planes // 2, planes)
            rows, cols = corner(z, 512 * c)
            to = (2 * zd + lax.rem(t, 2), seq)
            push(zres, zag.at[rows, cols], to, ssem.at[11], rsem.at[11])
            return carry

        lax.fori_loop(0, 2 * planes, spread, 0)
    else:
        zag[:, my_half] = (total * (1.0 / 256.0)).astype(BF)
        send(zag.at[:, my_half], zag.at[:, my_half], sibling, ssem.at[11], rsem.at[11])

    ring_forward(w_all, w_ssem, w_sem)
    ring_relay(w_all, w_ssem, w_sem)
    ring_far(w_all, w_ssem, w_sem)
    landed(att_ret, rsem.at[3])
    ring_rest(w_all, w_sem)
    done = jnp.dot(
        att_ret[...].reshape(2 * ROWS, WIDTH),
        w_all[...].reshape(WIDTH, WIDTH),
        preferred_element_type=F32,
    ).astype(BF)
    outgoing = []

    def write(i, src, dst):
        outgoing.append(pltpu.make_async_copy(src, dst, out_sem.at[i]))
        outgoing[-1].start()

    mixed_rows[3] = jnp.swapaxes(done.reshape(2, ROWS, WIDTH), 0, 1)
    write(3, mixed_rows.at[3], out_ref)
    for i, ref in ((2, dv_ref), (0, dq_ref), (1, dk_ref)):
        landed(dqkv_ret.at[i], rsem.at[4 + i])
        mixed_rows[i] = jnp.swapaxes(dqkv_ret[i], 0, 1)
        write(i, mixed_rows.at[i], ref)

    if planes > 1:
        landed(zag, rsem.at[11])
    else:
        landed(zag.at[:, pl.ds(pl.multiple_of(512 - 512 * c, 512), 512)], rsem.at[11])
    wg_f32[...] = zag[...].astype(F32)
    write(4, wg_f32, grad_ref)

    def left_here(sem, whole, short, is_short):
        @pl.when(is_short)
        def _():
            landed(short, sem)

        @pl.when(jnp.logical_not(is_short))
        def _():
            landed(whole, sem)

    @pl.when(own_side)
    def _():
        landed(aux, ssem.at[8])

    left_here(ssem.at[0], cot_s, cot_s.at[0], own_side)
    left_here(ssem.at[1], cot_s, cot_s.at[0], own_side)
    most = pl.ds(0, 15 * ROWS)
    left_here(ssem.at[2], qkv_r.at[0:2], qkv_r.at[0:2, most], own_side)
    left_here(ssem.at[9], qkv_r.at[2], qkv_r.at[2, most], own_side)
    left_here(ssem.at[3], att_n, att_n.at[most], own_side)
    for i in range(3):
        left_here(ssem.at[4 + i], dqkv_n.at[i], dqkv_n.at[i, most], own_side)
    left_here(ssem.at[7], ry, ry.at[pl.ds(0, 3)], own_side)
    if planes > 1:
        landed(zr.at[pl.ds(0, planes - 1)], ssem.at[10])
        landed(zr.at[pl.ds(0, planes - 1)], ssem.at[11])
        landed(zr, ssem.at[11])
    else:
        landed(zag.at[:, my_half], ssem.at[11])
    ring_drain(cot_all, cot_ssem)
    ring_drain(w_all, w_ssem)
    for copy in outgoing:
        copy.wait()


def finish(*refs):
    sem = refs[-1]
    copies = [pltpu.make_async_copy(refs[i], refs[5 + i], sem.at[i]) for i in range(5)]
    for copy in copies:
        copy.start()
    for copy in copies:
        copy.wait()


def on_device(queries, key_rows, value_rows, cotangent, out_weight, node_counts, edge_bits):
    planes = lax.axis_size("dp") // 2
    hbm = pl.BlockSpec(memory_space=pltpu.HBM)
    most_vmem = 60 * 1024 * 1024
    rows3 = jax.ShapeDtypeStruct((ROWS, 2, WIDTH), BF)
    grad = jax.ShapeDtypeStruct((ROWS, WIDTH), F32)
    dma = pltpu.SemaphoreType.DMA
    shapes = (rows3, rows3, rows3, rows3, grad)
    results = pl.pallas_call(
        functools.partial(kernel, planes),
        out_shape=shapes,
        in_specs=[hbm] * 7,
        out_specs=(hbm,) * 5,
        scratch_shapes=[
            pltpu.VMEM((4, ROWS, 2, WIDTH), BF),
            pltpu.VMEM((ROWS, WIDTH), BF),
            pltpu.SMEM((2,), jnp.int32),
            pltpu.SMEM((2, 8), jnp.int32),
            pltpu.VMEM((3, 2, ROWS, WIDTH), BF),
            pltpu.VMEM((2, ROWS, WIDTH), BF),
            pltpu.VMEM((3, NODES, HEAD), BF),
            pltpu.VMEM((16, NODES), F32),
            pltpu.VMEM((8, BLOCK, WIDTH), BF),
            pltpu.VMEM((8, BLOCK, WIDTH), BF),
            pltpu.VMEM((NODES, IB), F32),
            pltpu.VMEM((NODES // IB, NODES, IB), F32),
            pltpu.VMEM((NODES, NODES), BF),
            pltpu.VMEM((NODES, NODES), BF),
            pltpu.VMEM((HEAD, NODES), BF),
            pltpu.VMEM((NODES, HEAD), BF),
            pltpu.VMEM((NODES, HEAD), BF),
            pltpu.VMEM((HEAD, NODES), BF),
            pltpu.VMEM((HEAD, NODES), BF),
            pltpu.VMEM((HEAD, NODES), BF),
            pltpu.VMEM((3, NODES, HEAD), BF),
            pltpu.VMEM((2, ROWS, WIDTH), BF),
            pltpu.VMEM((3, 2, ROWS, WIDTH), BF),
            pltpu.VMEM((HEAD, WIDTH), BF),
            pltpu.VMEM((4, ROWS, 512), BF),
            pltpu.VMEM((ROWS, 512), BF),
            pltpu.VMEM((16, 16, 128), BF),
            pltpu.VMEM((16, 128), BF),
            pltpu.VMEM((ROWS, WIDTH), BF),
            pltpu.VMEM((4, ROWS, 2, WIDTH), BF),
            pltpu.VMEM((ROWS, WIDTH), F32),
            dma((7,)),
            dma((5,)),
            dma((12,)),
            dma((16,)),
            dma((14,)),
            dma((14,)),
            dma((14,)),
            dma((14,)),
        ],
        compiler_params=pltpu.CompilerParams(
            collective_id=0, has_side_effects=True, vmem_limit_bytes=most_vmem
        ),
        cost_estimate=pl.CostEstimate(
            flops=3_000_000_000, bytes_accessed=3_000_000, transcendentals=1_000_000
        ),
        name="sublayer",
    )(
        queries,
        key_rows,
        value_rows,
        cotangent,
        out_weight,
        node_counts,
        edge_bits.reshape(2, 8),
    )
    return pl.pallas_call(
        finish,
        out_shape=shapes,
        in_specs=[hbm] * 5,
        out_specs=(hbm,) * 5,
        scratch_shapes=[dma((5,))],
        compiler_params=pltpu.CompilerParams(vmem_limit_bytes=most_vmem),
        name="results",
    )(*results)


def solution(mesh):
    rows = P("seq", "dp", None)
    weight = P("seq", None)
    return jax.shard_map(
        on_device,
        mesh=mesh,
        in_specs=(rows, rows, rows, rows, weight, P("dp"), P("dp", None, None)),
        out_specs=(rows, rows, rows, rows, weight),
        check_vma=False,
    )
```

time: 87.9 us -> 112 us (1.27)
  Pallas kernels: 78.1 us -> 112 us
  local copies, waits for them, and re-layouts: 8.88 us -> 0 us
    pallas_call x1 -> x2, Pallas kernels: 78.1 us -> 112 us  [the longest x1 70.7 us: on_device(): pl.pallas_call(functools.partial(kernel, planes), out_shape=shapes, in_sp...]
    unnamed x19 -> x0, local copies, waits for them, and re-layouts: 8.88 us -> none
where the time goes in v2:
time: 112 us
  Pallas kernels  112 us (100%)
    pallas_call x1, Pallas kernels, on_device(): pl.pallas_call(functools.partial(kernel, planes), out_shape=shapes, in_sp...  70.7 us
    pallas_call x1, Pallas kernels, on_device(): pl.pallas_call(finish, out_shape=shapes, in_specs=[hbm] * 5, out_specs=(h...  40.9 us

profile of v2, /device:TPU:1, one launch (start us, length us, event | category | flops | bytes accessed | tf_op | source)
XLA Modules:
  0.0 112.2 jit_solution(8380906717698269068)
XLA Ops:
  0.6 70.7 %sublayer.1 = (bf16[64,2,1024]{2,1,0:T(2,128)(2,1)}, bf16[64,2,1024]{2,1,0:T(2,128)(2,1)}, bf16[64,2,1024]{2,1,0:T(2,128)(2,1)}, bf16[64,2,1024]{2,1,0:T(2,128)(2,1)}, f32[64,1024]{1,0:T(8,128)}) custom-call(bf16[64,2,1024]{2,1,0:T(2,128)(2,1)} %q_ref.1, bf16[64,2,1024]{2,1,0:T(2,128)(2,1)} %k_ref.1, bf16[64,2,1024]{2,1,0:T(2,128)(2,1)} %v_ref.1, ...), custom_call_target="tpu_custom_call" | custom-call | flops 3000000000 | bytes 3000000 | tf_op jit(solution)/shard_map/sublayer/pallas_call | solution.py:526
  71.3 40.9 %results.1 = (bf16[64,2,1024]{2,1,0:T(2,128)(2,1)}, bf16[64,2,1024]{2,1,0:T(2,128)(2,1)}, bf16[64,2,1024]{2,1,0:T(2,128)(2,1)}, bf16[64,2,1024]{2,1,0:T(2,128)(2,1)}, f32[64,1024]{1,0:T(8,128)}) custom-call(bf16[64,2,1024]{2,1,0:T(2,128)(2,1)} %get-tuple-element.10.refs_0_, bf16[64,2,1024]{2,1,0:T(2,128)(2,1)} %get-tuple-element.11.refs_1_, ...), custom_call_target="tpu_custom_call" | custom-call | tf_op jit(solution)/shard_map/results/pallas_call | solution.py:588

commit v3 on v2

--- a/solution.py
+++ b/solution.py
@@ -125,8 +125,7 @@
 
     def greet_z(t, carry):
         zd = lax.rem(z + t, planes)
-        greet((2 * zd, seq))
-        greet((2 * zd + 1, seq))
+        greet((2 * zd + c, seq))
         return carry
 
     if planes > 1:
@@ -146,11 +145,11 @@
 
     @pl.when(own_side)
     def _():
-        pl.semaphore_wait(barrier, 23 + 2 * (planes - 1))
+        pl.semaphore_wait(barrier, 23 + planes - 1)
 
     @pl.when(jnp.logical_not(own_side))
     def _():
-        pl.semaphore_wait(barrier, 26 + 2 * (planes - 1))
+        pl.semaphore_wait(barrier, 26 + planes - 1)
 
     def push(src, dst, to, s_sem, r_sem):
         same = (to[0] == dp) & (to[1] == seq)
@@ -351,20 +350,24 @@
     give_back(att_n, att_ret, ssem.at[3], rsem.at[3], 0, 16)
     ring_rest(cot_all, cot_sem)
 
-    part[...] = jnp.dot(
-        att_t[...], cot_all[...].reshape(NODES, WIDTH), preferred_element_type=F32
-    ).astype(BF)
-    for r in range(2):
+    cot_rows = cot_all[...].reshape(NODES, WIDTH)
+    for h in range(2):
         for cd in range(2):
-            push(
-                part.at[pl.ds(ROWS * r, ROWS), pl.ds(512 * cd, 512)],
-                ry.at[y],
-                dev(x, 2 * c + r, cd),
-                ssem.at[7],
-                rsem.at[7],
-            )
+            edge = 512 * cd + 256 * h
+            part[:, edge : edge + 256] = jnp.dot(
+                att_t[...], cot_rows[:, edge : edge + 256], preferred_element_type=F32
+            ).astype(BF)
+            for r in range(2):
+                push(
+                    part.at[pl.ds(ROWS * r, ROWS), pl.ds(edge, 256)],
+                    ry.at[h, y],
+                    dev(x, 2 * c + r, cd),
+                    ssem.at[7],
+                    rsem.at[7 if h == 0 else 10],
+                )
     landed(w_all.at[b_own, low], rsem.at[14])
     landed(w_all.at[b_own, high], rsem.at[15])
+    ring_own(w_all, w_ssem, w_sem)
     for b in range(8):
         rows = pl.ds(b * BLOCK, BLOCK)
         g = lax.dot_general(cot_all[b], w_all[b_own], NT, preferred_element_type=F32)
@@ -394,56 +397,59 @@
         give_back(dqkv_n.at[0], dqkv_ret.at[0], ssem.at[4], rsem.at[4], 4 * i, 4)
         return carry
 
-    lax.fori_loop(0, 2, backward, 0)
-
-    landed(ry, rsem.at[7])
-    total = ry[0].astype(F32) + ry[1].astype(F32) + ry[2].astype(F32) + ry[3].astype(F32)
-    zsrc[...] = total.astype(BF)
-
-    def corner(p, left_edge=0):
+    def corner(p, edge):
+        q = p // 2
         return (
-            pl.ds(pl.multiple_of(16 * (p // 4), 16), 16),
-            pl.ds(pl.multiple_of(left_edge + 128 * lax.rem(p, 4), 128), 128),
+            pl.ds(pl.multiple_of(16 * lax.rem(q, 4), 16), 16),
+            pl.ds(pl.multiple_of(edge + 128 * (q // 4), 128), 128),
         )
 
-    if planes > 1:
+    def to_planes(h):
+        landed(ry.at[h], rsem.at[7 if h == 0 else 10])
+        total = ry[h, 0].astype(F32) + ry[h, 1].astype(F32)
+        total = total + ry[h, 2].astype(F32) + ry[h, 3].astype(F32)
+        zsrc[h] = total.astype(BF)
+        if planes == 1:
+            zag[:, pl.ds(pl.multiple_of(512 * c + 256 * h, 256), 256)] = (
+                total * (1.0 / 256.0)
+            ).astype(BF)
+            return
 
         def send_z(t, carry):
-            zd = lax.rem(z + t + planes // 2, planes)
-            rows, cols = corner(zd)
-            push(zsrc.at[rows, cols], zr.at[z], (2 * zd + c, seq), ssem.at[10], rsem.at[10])
+            zd = 2 * lax.rem(z // 2 + t + 4, planes // 2) + h
+            rows, cols = corner(zd, 0)
+            push(zsrc.at[h, rows, cols], zr.at[z], (2 * zd + c, seq), ssem.at[10], rsem.at[16])
             return carry
 
-        lax.fori_loop(0, planes, send_z, 0)
-
+        lax.fori_loop(0, planes // 2, send_z, 0)
+
+    lax.fori_loop(0, 1, backward, 0)
+    to_planes(0)
+    lax.fori_loop(1, 2, backward, 0)
+    to_planes(1)
     lax.fori_loop(2, 4, backward, 0)
-
     dqkv_n[1] = jnp.dot(sgrad[...], qkv_r[0], preferred_element_type=F32).astype(BF)
     give_back(dqkv_n.at[1], dqkv_ret.at[1], ssem.at[5], rsem.at[5], 0, 16)
-    ring_own(w_all, w_ssem, w_sem)
-
-    my_half = pl.ds(pl.multiple_of(512 * c, 512), 512)
+    ring_forward(w_all, w_ssem, w_sem)
+    ring_relay(w_all, w_ssem, w_sem)
+
     if planes > 1:
-        landed(zr, rsem.at[10])
+        landed(zr, rsem.at[16])
         zsum = zr[0].astype(F32)
         for p in range(1, planes):
             zsum = zsum + zr[p].astype(F32)
         zres[...] = (zsum * (1.0 / 256.0)).astype(BF)
+        parity = lax.rem(z, 2)
+        rows, cols = corner(z, 512 * c + 256 * parity)
 
         def spread(t, carry):
-            zd = lax.rem(z + t // 2 + planes // 2, planes)
-            rows, cols = corner(z, 512 * c)
-            to = (2 * zd + lax.rem(t, 2), seq)
-            push(zres, zag.at[rows, cols], to, ssem.at[11], rsem.at[11])
+            zd = lax.rem(z + t + planes // 2, planes)
+            to = (2 * zd + c, seq)
+            push(zres, zag.at[rows, cols], to, ssem.at[11], rsem.at[17 + parity])
             return carry
 
-        lax.fori_loop(0, 2 * planes, spread, 0)
-    else:
-        zag[:, my_half] = (total * (1.0 / 256.0)).astype(BF)
-        send(zag.at[:, my_half], zag.at[:, my_half], sibling, ssem.at[11], rsem.at[11])
-
-    ring_forward(w_all, w_ssem, w_sem)
-    ring_relay(w_all, w_ssem, w_sem)
+        lax.fori_loop(0, planes, spread, 0)
+
     ring_far(w_all, w_ssem, w_sem)
     landed(att_ret, rsem.at[3])
     ring_rest(w_all, w_sem)
@@ -465,10 +471,13 @@
         mixed_rows[i] = jnp.swapaxes(dqkv_ret[i], 0, 1)
         write(i, mixed_rows.at[i], ref)
 
-    if planes > 1:
-        landed(zag, rsem.at[11])
-    else:
-        landed(zag.at[:, pl.ds(pl.multiple_of(512 - 512 * c, 512), 512)], rsem.at[11])
+    for h in range(2):
+        mine = zag.at[:, pl.ds(pl.multiple_of(512 * c + 256 * h, 256), 256)]
+        if planes > 1:
+            landed(mine, rsem.at[17 + h])
+        send(mine, mine, sibling, ssem.at[12 + h], rsem.at[19 + h])
+    for h in range(2):
+        landed(zag.at[:, pl.ds(pl.multiple_of(512 - 512 * c + 256 * h, 256), 256)], rsem.at[19 + h])
     wg_f32[...] = zag[...].astype(F32)
     write(4, wg_f32, grad_ref)
 
@@ -493,13 +502,12 @@
     left_here(ssem.at[3], att_n, att_n.at[most], own_side)
     for i in range(3):
         left_here(ssem.at[4 + i], dqkv_n.at[i], dqkv_n.at[i, most], own_side)
-    left_here(ssem.at[7], ry, ry.at[pl.ds(0, 3)], own_side)
+    left_here(ssem.at[7], ry, ry.at[:, pl.ds(0, 3)], own_side)
     if planes > 1:
         landed(zr.at[pl.ds(0, planes - 1)], ssem.at[10])
         landed(zr.at[pl.ds(0, planes - 1)], ssem.at[11])
-        landed(zr, ssem.at[11])
-    else:
-        landed(zag.at[:, my_half], ssem.at[11])
+    for h in range(2):
+        landed(zag.at[:, pl.ds(256 * h, 256)], ssem.at[12 + h])
     ring_drain(cot_all, cot_ssem)
     ring_drain(w_all, w_ssem)
     for copy in outgoing:
@@ -507,11 +515,15 @@
 
 
 def finish(*refs):
-    sem = refs[-1]
-    copies = [pltpu.make_async_copy(refs[i], refs[5 + i], sem.at[i]) for i in range(5)]
-    for copy in copies:
+    held, sem = refs[10:15], refs[15]
+    inward = [pltpu.make_async_copy(refs[i], held[i], sem.at[i]) for i in range(5)]
+    outward = [pltpu.make_async_copy(held[i], refs[5 + i], sem.at[5 + i]) for i in range(5)]
+    for copy in inward:
         copy.start()
-    for copy in copies:
+    for first, second in zip(inward, outward):
+        first.wait()
+        second.start()
+    for copy in outward:
         copy.wait()
 
 
@@ -553,8 +565,8 @@
             pltpu.VMEM((2, ROWS, WIDTH), BF),
             pltpu.VMEM((3, 2, ROWS, WIDTH), BF),
             pltpu.VMEM((HEAD, WIDTH), BF),
-            pltpu.VMEM((4, ROWS, 512), BF),
-            pltpu.VMEM((ROWS, 512), BF),
+            pltpu.VMEM((2, 4, ROWS, 256), BF),
+            pltpu.VMEM((2, ROWS, 256), BF),
             pltpu.VMEM((16, 16, 128), BF),
             pltpu.VMEM((16, 128), BF),
             pltpu.VMEM((ROWS, WIDTH), BF),
@@ -562,8 +574,8 @@
             pltpu.VMEM((ROWS, WIDTH), F32),
             dma((7,)),
             dma((5,)),
-            dma((12,)),
-            dma((16,)),
+            dma((14,)),
+            dma((21,)),
             dma((14,)),
             dma((14,)),
             dma((14,)),
@@ -590,7 +602,7 @@
         out_shape=shapes,
         in_specs=[hbm] * 5,
         out_specs=(hbm,) * 5,
-        scratch_shapes=[dma((5,))],
+        scratch_shapes=[pltpu.VMEM(one.shape, one.dtype) for one in shapes] + [dma((10,))],
         compiler_params=pltpu.CompilerParams(vmem_limit_bytes=most_vmem),
         name="results",
     )(*results)

time: 112 us -> 70.1 us (0.63)
  Pallas kernels: 112 us -> 69.3 us
    pallas_call x1, Pallas kernels: 40.9 us -> 2.09 us  [on_device(): pl.pallas_call(finish, out_shape=shapes, in_specs=[hbm] * 5, out_specs=(h...]
    pallas_call x1, Pallas kernels: 70.7 us -> 67.2 us  [on_device(): pl.pallas_call(functools.partial(kernel, planes), out_shape=shapes, in_sp...]
where the time goes in v3:
time: 70.1 us; the launch traced here: 69.9 us
  Pallas kernels  69.3 us (99%)
    pallas_call x1, Pallas kernels, on_device(): pl.pallas_call(functools.partial(kernel, planes), out_shape=shapes, in_sp...  67.2 us
    pallas_call x1, Pallas kernels, on_device(): pl.pallas_call(finish, out_shape=shapes, in_specs=[hbm] * 5, out_specs=(h...  2.09 us

profile of v3, /device:TPU:1, one launch (start us, length us, event | category | flops | bytes accessed | tf_op | source)
XLA Modules:
  0.0 69.9 jit_solution(67367518920489820)
XLA Ops:
  0.6 67.2 %sublayer.1 = (bf16[64,2,1024]{2,1,0:T(2,128)(2,1)}, bf16[64,2,1024]{2,1,0:T(2,128)(2,1)}, bf16[64,2,1024]{2,1,0:T(2,128)(2,1)}, bf16[64,2,1024]{2,1,0:T(2,128)(2,1)}, f32[64,1024]{1,0:T(8,128)}) custom-call(bf16[64,2,1024]{2,1,0:T(2,128)(2,1)} %q_ref.1, bf16[64,2,1024]{2,1,0:T(2,128)(2,1)} %k_ref.1, bf16[64,2,1024]{2,1,0:T(2,128)(2,1)} %v_ref.1, ...), custom_call_target="tpu_custom_call" | custom-call | flops 3000000000 | bytes 3000000 | tf_op jit(solution)/shard_map/sublayer/pallas_call | solution.py:538
  67.8 2.1 %results.1 = (bf16[64,2,1024]{2,1,0:T(2,128)(2,1)}, bf16[64,2,1024]{2,1,0:T(2,128)(2,1)}, bf16[64,2,1024]{2,1,0:T(2,128)(2,1)}, bf16[64,2,1024]{2,1,0:T(2,128)(2,1)}, f32[64,1024]{1,0:T(8,128)}) custom-call(bf16[64,2,1024]{2,1,0:T(2,128)(2,1)} %get-tuple-element.10.refs_0_, bf16[64,2,1024]{2,1,0:T(2,128)(2,1)} %get-tuple-element.11.refs_1_, ...), custom_call_target="tpu_custom_call" | custom-call | tf_op jit(solution)/shard_map/results/pallas_call | solution.py:600

commit v4 on v3

--- a/solution.py
+++ b/solution.py
@@ -74,6 +74,7 @@
     w_sem,
     cot_ssem,
     w_ssem,
+    known,
 ):
     dp = lax.axis_index("dp")
     seq = lax.axis_index("seq")
@@ -123,13 +124,15 @@
 
         return carry
 
-    def greet_z(t, carry):
-        zd = lax.rem(z + t, planes)
-        greet((2 * zd + c, seq))
-        return carry
+    def planes_at(distance):
+        return (
+            (2 * lax.rem(z + distance, planes) + c, seq),
+            (2 * lax.rem(z + planes - distance, planes) + c, seq),
+        )
 
     if planes > 1:
-        lax.fori_loop(1, planes, greet_z, 0)
+        for to in planes_at(1):
+            greet(to)
     lax.fori_loop(0, 16, greet_plane, 0)
 
     @pl.when(jnp.logical_not(own_side))
@@ -143,13 +146,28 @@
         incoming[1 + i].wait()
         qkv_s[i] = jnp.swapaxes(raw[i], 0, 1)
 
+    greeted = 2 if planes > 1 else 0
+
     @pl.when(own_side)
     def _():
-        pl.semaphore_wait(barrier, 23 + planes - 1)
+        pl.semaphore_wait(barrier, 23 + greeted)
 
     @pl.when(jnp.logical_not(own_side))
     def _():
-        pl.semaphore_wait(barrier, 26 + planes - 1)
+        pl.semaphore_wait(barrier, 26 + greeted)
+
+    def tell(step):
+        if planes > 1:
+            for to in planes_at(2**step):
+                pl.semaphore_signal(known.at[step], inc=1, device_id=to, device_id_type=MESH)
+
+    def learn(step):
+        if planes > 1:
+            pl.semaphore_wait(known.at[step], 2)
+            if step < 2:
+                tell(step + 1)
+
+    tell(0)
 
     def push(src, dst, to, s_sem, r_sem):
         same = (to[0] == dp) & (to[1] == seq)
@@ -273,6 +291,7 @@
     landed(cot_all.at[b_own, high], rsem.at[13])
     ring_own(cot_all, cot_ssem, cot_sem)
     ring_forward(cot_all, cot_ssem, cot_sem)
+    learn(0)
 
     @pl.when(jnp.logical_not(own_side))
     def _():
@@ -315,6 +334,7 @@
         return carry
 
     lax.fori_loop(0, 4, forward, 0)
+    learn(1)
     ring_relay(cot_all, cot_ssem, cot_sem)
     kt[...] = qkv_r[1].astype(F32).T.astype(BF)
     landed(qkv_r.at[pl.ds(2, 1)], rsem.at[9])
@@ -347,7 +367,6 @@
         lax.fori_loop(0, count, one, 0)
 
     ring_far(cot_all, cot_ssem, cot_sem)
-    give_back(att_n, att_ret, ssem.at[3], rsem.at[3], 0, 16)
     ring_rest(cot_all, cot_sem)
 
     cot_rows = cot_all[...].reshape(NODES, WIDTH)
@@ -376,7 +395,6 @@
         ag_n[rows, :] = gt.T.astype(BF)
 
     dqkv_n[2] = jnp.dot(prob_b[...], ag_n[...], preferred_element_type=F32).astype(BF)
-    give_back(dqkv_n.at[2], dqkv_ret.at[2], ssem.at[6], rsem.at[6], 0, 16)
 
     scale = 1.0 / math.sqrt(HEAD)
 
@@ -394,6 +412,10 @@
             sgrad[rows, here] = (prob[i, rows, :] * ((pg - centre) * scale)).astype(BF)
         dq = jnp.dot(kt[...], sgrad[:, here], preferred_element_type=F32)
         dqkv_n[0, here, :] = dq.T.astype(BF)
+        return carry
+
+    def return_dq(step, carry):
+        i = lax.rem(x + step, 4)
         give_back(dqkv_n.at[0], dqkv_ret.at[0], ssem.at[4], rsem.at[4], 4 * i, 4)
         return carry
 
@@ -424,14 +446,18 @@
         lax.fori_loop(0, planes // 2, send_z, 0)
 
     lax.fori_loop(0, 1, backward, 0)
+    learn(2)
     to_planes(0)
     lax.fori_loop(1, 2, backward, 0)
     to_planes(1)
+    give_back(dqkv_n.at[2], dqkv_ret.at[2], ssem.at[6], rsem.at[6], 0, 16)
+    lax.fori_loop(0, 2, return_dq, 0)
     lax.fori_loop(2, 4, backward, 0)
+    lax.fori_loop(2, 4, return_dq, 0)
     dqkv_n[1] = jnp.dot(sgrad[...], qkv_r[0], preferred_element_type=F32).astype(BF)
     give_back(dqkv_n.at[1], dqkv_ret.at[1], ssem.at[5], rsem.at[5], 0, 16)
+    give_back(att_n, att_ret, ssem.at[3], rsem.at[3], 0, 16)
     ring_forward(w_all, w_ssem, w_sem)
-    ring_relay(w_all, w_ssem, w_sem)
 
     if planes > 1:
         landed(zr, rsem.at[16])
@@ -450,6 +476,7 @@
 
         lax.fori_loop(0, planes, spread, 0)
 
+    ring_relay(w_all, w_ssem, w_sem)
     ring_far(w_all, w_ssem, w_sem)
     landed(att_ret, rsem.at[3])
     ring_rest(w_all, w_sem)
@@ -580,6 +607,7 @@
             dma((14,)),
             dma((14,)),
             dma((14,)),
+            pltpu.SemaphoreType.REGULAR((3,)),
         ],
         compiler_params=pltpu.CompilerParams(
             collective_id=0, has_side_effects=True, vmem_limit_bytes=most_vmem

time: 70.1 us -> 68.7 us (0.980)
  Pallas kernels: 69.3 us -> 67.9 us
    pallas_call x1, Pallas kernels: 67.2 us -> 65.8 us  [on_device(): pl.pallas_call(functools.partial(kernel, planes), out_shape=shapes, in_sp...]
where the time goes in v4:
time: 68.7 us; the launch traced here: 68.6 us
  Pallas kernels  67.9 us (99%)
    pallas_call x1, Pallas kernels, on_device(): pl.pallas_call(functools.partial(kernel, planes), out_shape=shapes, in_sp...  65.8 us
    pallas_call x1, Pallas kernels, on_device(): pl.pallas_call(finish, out_shape=shapes, in_specs=[hbm] * 5, out_specs=(h...  2.09 us

profile of v4, /device:TPU:1, one launch (start us, length us, event | category | flops | bytes accessed | tf_op | source)
XLA Modules:
  0.0 68.6 jit_solution(16095646095740320296)
XLA Ops:
  0.6 65.8 %sublayer.1 = (bf16[64,2,1024]{2,1,0:T(2,128)(2,1)}, bf16[64,2,1024]{2,1,0:T(2,128)(2,1)}, bf16[64,2,1024]{2,1,0:T(2,128)(2,1)}, bf16[64,2,1024]{2,1,0:T(2,128)(2,1)}, f32[64,1024]{1,0:T(8,128)}) custom-call(bf16[64,2,1024]{2,1,0:T(2,128)(2,1)} %q_ref.1, bf16[64,2,1024]{2,1,0:T(2,128)(2,1)} %k_ref.1, bf16[64,2,1024]{2,1,0:T(2,128)(2,1)} %v_ref.1, ...), custom_call_target="tpu_custom_call" | custom-call | flops 3000000000 | bytes 3000000 | tf_op jit(solution)/shard_map/sublayer/pallas_call | solution.py:565
  66.5 2.1 %results.1 = (bf16[64,2,1024]{2,1,0:T(2,128)(2,1)}, bf16[64,2,1024]{2,1,0:T(2,128)(2,1)}, bf16[64,2,1024]{2,1,0:T(2,128)(2,1)}, bf16[64,2,1024]{2,1,0:T(2,128)(2,1)}, f32[64,1024]{1,0:T(8,128)}) custom-call(bf16[64,2,1024]{2,1,0:T(2,128)(2,1)} %get-tuple-element.10.refs_0_, bf16[64,2,1024]{2,1,0:T(2,128)(2,1)} %get-tuple-element.11.refs_1_, ...), custom_call_target="tpu_custom_call" | custom-call | tf_op jit(solution)/shard_map/results/pallas_call | solution.py:628

commit v5 on v4

--- a/solution.py
+++ b/solution.py
@@ -230,6 +230,11 @@
             aux[8:16, i * BLOCK : (i + 1) * BLOCK] = jnp.where(live, 1.0, 0.0)
         send(aux, aux, sibling, ssem.at[8], rsem.at[8])
 
+    incoming[4].wait()
+    for j in range(2):
+        to = dev(x, 2 * c + j, y // 2)
+        push(w_ref, w_all.at[2 * x + y // 2, half], to, ssem.at[1], rsem.at[14 + y % 2])
+
     right = dev(lax.rem(x + 1, 4), y, c)
     left = dev(lax.rem(x + 3, 4), y, c)
     b_own = head
@@ -298,11 +303,6 @@
         landed(aux, rsem.at[8])
 
     landed(qkv_r.at[pl.ds(0, 2)], rsem.at[2])
-
-    incoming[4].wait()
-    for j in range(2):
-        to = dev(x, 2 * c + j, y // 2)
-        push(w_ref, w_all.at[2 * x + y // 2, half], to, ssem.at[1], rsem.at[14 + y % 2])
 
     factor = math.log2(math.e) / math.sqrt(HEAD)
     key_pos = lax.broadcasted_iota(jnp.int32, (BLOCK, IB), 0).astype(F32)
@@ -336,6 +336,9 @@
     lax.fori_loop(0, 4, forward, 0)
     learn(1)
     ring_relay(cot_all, cot_ssem, cot_sem)
+    landed(w_all.at[b_own, low], rsem.at[14])
+    landed(w_all.at[b_own, high], rsem.at[15])
+    ring_own(w_all, w_ssem, w_sem)
     kt[...] = qkv_r[1].astype(F32).T.astype(BF)
     landed(qkv_r.at[pl.ds(2, 1)], rsem.at[9])
     vt[...] = qkv_r[2].astype(F32).T.astype(BF)
@@ -384,9 +387,6 @@
                     ssem.at[7],
                     rsem.at[7 if h == 0 else 10],
                 )
-    landed(w_all.at[b_own, low], rsem.at[14])
-    landed(w_all.at[b_own, high], rsem.at[15])
-    ring_own(w_all, w_ssem, w_sem)
     for b in range(8):
         rows = pl.ds(b * BLOCK, BLOCK)
         g = lax.dot_general(cot_all[b], w_all[b_own], NT, preferred_element_type=F32)
@@ -394,6 +394,7 @@
         ag_t[:, rows] = gt.astype(BF)
         ag_n[rows, :] = gt.T.astype(BF)
 
+    give_back(att_n, att_ret, ssem.at[3], rsem.at[3], 0, 16)
     dqkv_n[2] = jnp.dot(prob_b[...], ag_n[...], preferred_element_type=F32).astype(BF)
 
     scale = 1.0 / math.sqrt(HEAD)
@@ -448,16 +449,16 @@
     lax.fori_loop(0, 1, backward, 0)
     learn(2)
     to_planes(0)
+    give_back(dqkv_n.at[2], dqkv_ret.at[2], ssem.at[6], rsem.at[6], 0, 16)
+    ring_forward(w_all, w_ssem, w_sem)
     lax.fori_loop(1, 2, backward, 0)
     to_planes(1)
-    give_back(dqkv_n.at[2], dqkv_ret.at[2], ssem.at[6], rsem.at[6], 0, 16)
+    ring_relay(w_all, w_ssem, w_sem)
     lax.fori_loop(0, 2, return_dq, 0)
     lax.fori_loop(2, 4, backward, 0)
     lax.fori_loop(2, 4, return_dq, 0)
     dqkv_n[1] = jnp.dot(sgrad[...], qkv_r[0], preferred_element_type=F32).astype(BF)
     give_back(dqkv_n.at[1], dqkv_ret.at[1], ssem.at[5], rsem.at[5], 0, 16)
-    give_back(att_n, att_ret, ssem.at[3], rsem.at[3], 0, 16)
-    ring_forward(w_all, w_ssem, w_sem)
 
     if planes > 1:
         landed(zr, rsem.at[16])
@@ -476,7 +477,6 @@
 
         lax.fori_loop(0, planes, spread, 0)
 
-    ring_relay(w_all, w_ssem, w_sem)
     ring_far(w_all, w_ssem, w_sem)
     landed(att_ret, rsem.at[3])
     ring_rest(w_all, w_sem)

time: 68.7 us -> 65.2 us (0.949)
  the two profiles are of different devices: /device:TPU:1 before, /device:TPU:19 now
where the time goes in v5:
time: 65.2 us; the launch traced here: 65 us
  Pallas kernels  64.4 us (99%)
    pallas_call x1, Pallas kernels, on_device(): pl.pallas_call(functools.partial(kernel, planes), out_shape=shapes, in_sp...  62.3 us
    pallas_call x1, Pallas kernels, on_device(): pl.pallas_call(finish, out_shape=shapes, in_specs=[hbm] * 5, out_specs=(h...  2.09 us

profile of v5, /device:TPU:19, one launch (start us, length us, event | category | flops | bytes accessed | tf_op | source)
XLA Modules:
  0.0 65.0 jit_solution(3699138414931578139)
XLA Ops:
  0.6 62.3 %sublayer.1 = (bf16[64,2,1024]{2,1,0:T(2,128)(2,1)}, bf16[64,2,1024]{2,1,0:T(2,128)(2,1)}, bf16[64,2,1024]{2,1,0:T(2,128)(2,1)}, bf16[64,2,1024]{2,1,0:T(2,128)(2,1)}, f32[64,1024]{1,0:T(8,128)}) custom-call(bf16[64,2,1024]{2,1,0:T(2,128)(2,1)} %q_ref.1, bf16[64,2,1024]{2,1,0:T(2,128)(2,1)} %k_ref.1, bf16[64,2,1024]{2,1,0:T(2,128)(2,1)} %v_ref.1, ...), custom_call_target="tpu_custom_call" | custom-call | flops 3000000000 | bytes 3000000 | tf_op jit(solution)/shard_map/sublayer/pallas_call | solution.py:565
  62.9 2.1 %results.1 = (bf16[64,2,1024]{2,1,0:T(2,128)(2,1)}, bf16[64,2,1024]{2,1,0:T(2,128)(2,1)}, bf16[64,2,1024]{2,1,0:T(2,128)(2,1)}, bf16[64,2,1024]{2,1,0:T(2,128)(2,1)}, f32[64,1024]{1,0:T(8,128)}) custom-call(bf16[64,2,1024]{2,1,0:T(2,128)(2,1)} %get-tuple-element.10.refs_0_, bf16[64,2,1024]{2,1,0:T(2,128)(2,1)} %get-tuple-element.11.refs_1_, ...), custom_call_target="tpu_custom_call" | custom-call | tf_op jit(solution)/shard_map/results/pallas_call | solution.py:628

commit v6 on v5

--- a/solution.py
+++ b/solution.py
@@ -64,10 +64,7 @@
     zr,
     zres,
     zag,
-    mixed_rows,
-    wg_f32,
     in_sem,
-    out_sem,
     ssem,
     rsem,
     cot_sem,
@@ -357,7 +354,7 @@
 
     def give_back(src, dst, s_sem, r_sem, first, count):
         def one(t, carry):
-            to = first + t if count < 16 else lax.rem(seq + t, 16)
+            to = first + lax.rem(t + y + 2, 4) if count < 16 else lax.rem(seq + t + 8, 16)
             push(
                 src.at[pl.ds(pl.multiple_of(ROWS * to, ROWS), ROWS), :],
                 dst.at[y % 2, :, my_cols],
@@ -400,7 +397,7 @@
     scale = 1.0 / math.sqrt(HEAD)
 
     def backward(step, carry):
-        i = lax.rem(x + step, 4)
+        i = lax.rem(x + step + 2, 4)
         at = pl.multiple_of(i * IB, IB)
         here = pl.ds(at, IB)
         g_part = ag_n[here, :]
@@ -416,7 +413,7 @@
         return carry
 
     def return_dq(step, carry):
-        i = lax.rem(x + step, 4)
+        i = lax.rem(x + step + 2, 4)
         give_back(dqkv_n.at[0], dqkv_ret.at[0], ssem.at[4], rsem.at[4], 4 * i, 4)
         return carry
 
@@ -485,18 +482,10 @@
         w_all[...].reshape(WIDTH, WIDTH),
         preferred_element_type=F32,
     ).astype(BF)
-    outgoing = []
-
-    def write(i, src, dst):
-        outgoing.append(pltpu.make_async_copy(src, dst, out_sem.at[i]))
-        outgoing[-1].start()
-
-    mixed_rows[3] = jnp.swapaxes(done.reshape(2, ROWS, WIDTH), 0, 1)
-    write(3, mixed_rows.at[3], out_ref)
+    out_ref[...] = jnp.swapaxes(done.reshape(2, ROWS, WIDTH), 0, 1)
     for i, ref in ((2, dv_ref), (0, dq_ref), (1, dk_ref)):
         landed(dqkv_ret.at[i], rsem.at[4 + i])
-        mixed_rows[i] = jnp.swapaxes(dqkv_ret[i], 0, 1)
-        write(i, mixed_rows.at[i], ref)
+        ref[...] = jnp.swapaxes(dqkv_ret[i], 0, 1)
 
     for h in range(2):
         mine = zag.at[:, pl.ds(pl.multiple_of(512 * c + 256 * h, 256), 256)]
@@ -505,8 +494,7 @@
         send(mine, mine, sibling, ssem.at[12 + h], rsem.at[19 + h])
     for h in range(2):
         landed(zag.at[:, pl.ds(pl.multiple_of(512 - 512 * c + 256 * h, 256), 256)], rsem.at[19 + h])
-    wg_f32[...] = zag[...].astype(F32)
-    write(4, wg_f32, grad_ref)
+    grad_ref[...] = zag[...].astype(F32)
 
     def left_here(sem, whole, short, is_short):
         @pl.when(is_short)
@@ -537,36 +525,31 @@
         landed(zag.at[:, pl.ds(256 * h, 256)], ssem.at[12 + h])
     ring_drain(cot_all, cot_ssem)
     ring_drain(w_all, w_ssem)
-    for copy in outgoing:
-        copy.wait()
 
 
 def finish(*refs):
-    held, sem = refs[10:15], refs[15]
-    inward = [pltpu.make_async_copy(refs[i], held[i], sem.at[i]) for i in range(5)]
-    outward = [pltpu.make_async_copy(held[i], refs[5 + i], sem.at[5 + i]) for i in range(5)]
-    for copy in inward:
+    sem = refs[10]
+    copies = [pltpu.make_async_copy(refs[i], refs[5 + i], sem.at[i]) for i in range(5)]
+    for copy in copies:
         copy.start()
-    for first, second in zip(inward, outward):
-        first.wait()
-        second.start()
-    for copy in outward:
+    for copy in copies:
         copy.wait()
 
 
 def on_device(queries, key_rows, value_rows, cotangent, out_weight, node_counts, edge_bits):
     planes = lax.axis_size("dp") // 2
     hbm = pl.BlockSpec(memory_space=pltpu.HBM)
-    most_vmem = 60 * 1024 * 1024
+    vmem = pl.BlockSpec(memory_space=pltpu.VMEM)
+    most_vmem = 48 * 1024 * 1024
     rows3 = jax.ShapeDtypeStruct((ROWS, 2, WIDTH), BF)
     grad = jax.ShapeDtypeStruct((ROWS, WIDTH), F32)
     dma = pltpu.SemaphoreType.DMA
     shapes = (rows3, rows3, rows3, rows3, grad)
     results = pl.pallas_call(
         functools.partial(kernel, planes),
-        out_shape=shapes,
+        out_shape=tuple(pltpu.VMEM(one.shape, one.dtype) for one in shapes),
         in_specs=[hbm] * 7,
-        out_specs=(hbm,) * 5,
+        out_specs=(vmem,) * 5,
         scratch_shapes=[
             pltpu.VMEM((4, ROWS, 2, WIDTH), BF),
             pltpu.VMEM((ROWS, WIDTH), BF),
@@ -597,10 +580,7 @@
             pltpu.VMEM((16, 16, 128), BF),
             pltpu.VMEM((16, 128), BF),
             pltpu.VMEM((ROWS, WIDTH), BF),
-            pltpu.VMEM((4, ROWS, 2, WIDTH), BF),
-            pltpu.VMEM((ROWS, WIDTH), F32),
             dma((7,)),
-            dma((5,)),
             dma((14,)),
             dma((21,)),
             dma((14,)),
@@ -617,20 +597,25 @@
         ),
         name="sublayer",
     )(
-        queries,
-        key_rows,
-        value_rows,
-        cotangent,
-        out_weight,
-        node_counts,
-        edge_bits.reshape(2, 8),
+        *[
+            pltpu.with_memory_space_constraint(one, pltpu.HBM)
+            for one in (
+                queries,
+                key_rows,
+                value_rows,
+                cotangent,
+                out_weight,
+                node_counts,
+                edge_bits.reshape(2, 8),
+            )
+        ]
     )
     return pl.pallas_call(
         finish,
         out_shape=shapes,
-        in_specs=[hbm] * 5,
+        in_specs=[vmem] * 5,
         out_specs=(hbm,) * 5,
-        scratch_shapes=[pltpu.VMEM(one.shape, one.dtype) for one in shapes] + [dma((10,))],
+        scratch_shapes=[dma((5,))],
         compiler_params=pltpu.CompilerParams(vmem_limit_bytes=most_vmem),
         name="results",
     )(*results)

time: 65.2 us -> 63.3 us (0.971)
  the two profiles are of different devices: /device:TPU:19 before, /device:TPU:23 now
where the time goes in v6:
time: 63.3 us; the launch traced here: 63.2 us
  Pallas kernels  62.5 us (99%)
  between operations  0.64 us (1%)
    pallas_call x1, Pallas kernels, on_device(): pl.pallas_call(functools.partial(kernel, planes), out_shape=tuple((pltpu....  61.4 us

profile of v6, /device:TPU:23, one launch (start us, length us, event | category | flops | bytes accessed | tf_op | source)
XLA Modules:
  0.0 63.2 jit_solution(313550763894993117)
XLA Ops:
  0.6 61.4 %sublayer.1 = (bf16[64,2,1024]{2,1,0:T(2,128)(2,1)S(1)}, bf16[64,2,1024]{2,1,0:T(2,128)(2,1)S(1)}, bf16[64,2,1024]{2,1,0:T(2,128)(2,1)S(1)}, bf16[64,2,1024]{2,1,0:T(2,128)(2,1)S(1)}, f32[64,1024]{1,0:T(8,128)S(1)}) custom-call(bf16[64,2,1024]{2,1,0:T(2,128)(2,1)} %q_ref.1, bf16[64,2,1024]{2,1,0:T(2,128)(2,1)} %k_ref.1, bf16[64,2,1024]{2,1,0:T(2,128)(2,1)} %v_ref.1, ...), custom_call_target="tpu_custom_call" | custom-call | flops 3000000000 | bytes 3000000 | tf_op jit(solution)/shard_map/sublayer/pallas_call | solution.py:548
  62.1 1.1 %results.1 = (bf16[64,2,1024]{2,1,0:T(2,128)(2,1)}, bf16[64,2,1024]{2,1,0:T(2,128)(2,1)}, bf16[64,2,1024]{2,1,0:T(2,128)(2,1)}, bf16[64,2,1024]{2,1,0:T(2,128)(2,1)}, f32[64,1024]{1,0:T(8,128)}) custom-call(bf16[64,2,1024]{2,1,0:T(2,128)(2,1)S(1)} %get-tuple-element.10.refs_0_, bf16[64,2,1024]{2,1,0:T(2,128)(2,1)S(1)} %get-tuple-element.11.refs_1_, ...), custom_call_target="tpu_custom_call" | custom-call | tf_op jit(solution)/shard_map/results/pallas_call | solution.py:613

commit v7 on v6

--- a/solution.py
+++ b/solution.py
@@ -394,6 +394,8 @@
     give_back(att_n, att_ret, ssem.at[3], rsem.at[3], 0, 16)
     dqkv_n[2] = jnp.dot(prob_b[...], ag_n[...], preferred_element_type=F32).astype(BF)
 
+    give_back(dqkv_n.at[2], dqkv_ret.at[2], ssem.at[6], rsem.at[6], 0, 16)
+
     scale = 1.0 / math.sqrt(HEAD)
 
     def backward(step, carry):
@@ -446,7 +448,6 @@
     lax.fori_loop(0, 1, backward, 0)
     learn(2)
     to_planes(0)
-    give_back(dqkv_n.at[2], dqkv_ret.at[2], ssem.at[6], rsem.at[6], 0, 16)
     ring_forward(w_all, w_ssem, w_sem)
     lax.fori_loop(1, 2, backward, 0)
     to_planes(1)

time: 63.3 us -> 63.1 us (level)
  the two profiles are of different devices: /device:TPU:23 before, /device:TPU:7 now
where the time goes in v7:
time: 63.1 us; the launch traced here: 62.9 us
  Pallas kernels  62.3 us (99%)
  between operations  0.64 us (1%)
    pallas_call x1, Pallas kernels, on_device(): pl.pallas_call(functools.partial(kernel, planes), out_shape=tuple((pltpu....  61.2 us

profile of v7, /device:TPU:7, one launch (start us, length us, event | category | flops | bytes accessed | tf_op | source)
XLA Modules:
  0.0 62.9 jit_solution(15568866140523721958)
XLA Ops:
  0.6 61.2 %sublayer.1 = (bf16[64,2,1024]{2,1,0:T(2,128)(2,1)S(1)}, bf16[64,2,1024]{2,1,0:T(2,128)(2,1)S(1)}, bf16[64,2,1024]{2,1,0:T(2,128)(2,1)S(1)}, bf16[64,2,1024]{2,1,0:T(2,128)(2,1)S(1)}, f32[64,1024]{1,0:T(8,128)S(1)}) custom-call(bf16[64,2,1024]{2,1,0:T(2,128)(2,1)} %q_ref.1, bf16[64,2,1024]{2,1,0:T(2,128)(2,1)} %k_ref.1, bf16[64,2,1024]{2,1,0:T(2,128)(2,1)} %v_ref.1, ...), custom_call_target="tpu_custom_call" | custom-call | flops 3000000000 | bytes 3000000 | tf_op jit(solution)/shard_map/sublayer/pallas_call | solution.py:549
  61.9 1.1 %results.1 = (bf16[64,2,1024]{2,1,0:T(2,128)(2,1)}, bf16[64,2,1024]{2,1,0:T(2,128)(2,1)}, bf16[64,2,1024]{2,1,0:T(2,128)(2,1)}, bf16[64,2,1024]{2,1,0:T(2,128)(2,1)}, f32[64,1024]{1,0:T(8,128)}) custom-call(bf16[64,2,1024]{2,1,0:T(2,128)(2,1)S(1)} %get-tuple-element.10.refs_0_, bf16[64,2,1024]{2,1,0:T(2,128)(2,1)S(1)} %get-tuple-element.11.refs_1_, ...), custom_call_target="tpu_custom_call" | custom-call | tf_op jit(solution)/shard_map/results/pallas_call | solution.py:614
